TPU v7x, 256 devices: a whole 4x4x8 slice. The times are simulated.
256 devices in a mesh: ctx: 16 (over z_lo, y), tp: 8 (over x, core), pd: 2 (over z_hi).
Axes of the slice: x: 4, y: 4, z: 8 (z_hi: 2, z_lo: 4; z = z_hi * 4 + z_lo), core: 2. Of those that a mesh axis runs over, the one named last changes fastest.
Arguments:
- prefill_query: bfloat16 [2, 2, 4096, 8192], P('pd', None, 'ctx', 'tp'), may hold values from -24 to 24
- prefill_kv: bfloat16 [2, 2, 4096, 2048], P('pd', None, 'ctx', 'tp'), may hold values from -8 to 8
- decode_query: bfloat16 [2, 16, 16, 4, 8192], P('pd', 'ctx', None, None, 'tp'), may hold values from -24 to 24
- gen_cache: bfloat16 [2, 16, 16, 256, 2048], P('pd', 'ctx', None, None, 'tp'), may hold values from -8 to 8
- new_hidden: bfloat16 [2, 16, 16, 4, 8192], P('pd', 'ctx', None, None, 'tp'), may hold values from -6 to 6
- norm_gain: float32 [8192], replicated, may hold values from 0.1 to 1.9
- kv_weight: bfloat16 [8192, 2048], P(None, 'tp'), may hold values from -0.125 to 0.125
- prompt_of: int32 [2, 16], replicated, may hold values from 0 to 1, as said below
- cached_len: int32 [2, 16, 16], P('pd', 'ctx'), may hold values from 64 to 256, as said below
Outputs:
- segment_attention: bfloat16 [2, 2, 4096, 8192], P('pd', None, 'ctx', 'tp')
- decode_attention: bfloat16 [2, 16, 16, 4, 8192], P('pd', 'ctx', None, None, 'tp')
Inputs may be any that keep to these rules, and one draw needn't show every extreme that they name: `prompt_of`: in each pool every prompt is named by exactly 8 replicas. `cached_len`: in every pool and replica some completion holds exactly 256 slots and another exactly 64.
All inputs are finite; a program needn't handle non-finite values.
Results may differ from a plain program's by a relative error of at most 0.005.
Values may be sent and summed in bfloat16 or wider, within the bound.
No kernel may reach another device: no remote copies, remote signals or barrier semaphores. Data moves between devices by JAX's collectives and lax.ppermute only.
A program may use at most 192 MiB of HBM per device.

v0:
```python
import jax
import jax.numpy as jnp
from jax import lax
from jax.sharding import PartitionSpec as P

D = 8192
HD = 128
GROUP = 8


masked_score = -1e30


def shifted(block, axis, distance):
    devices = range(lax.axis_size(axis))
    route = [((i - distance) % len(devices), i) for i in devices]
    return lax.ppermute(block, axis, route)


def rotate_keys(key_rows, positions):
    half_dim = HD // 2
    frequency = 1000000.0 ** (-jnp.arange(half_dim, dtype=jnp.float32) * 2.0 / HD)
    angles = positions[..., None] * frequency
    first_half = key_rows[..., :half_dim]
    second_half = key_rows[..., half_dim:]
    cosine = jnp.cos(angles)
    sine_part = jnp.sin(angles)
    return jnp.concatenate(
        [
            first_half * cosine - second_half * sine_part,
            second_half * cosine + first_half * sine_part,
        ],
        axis=-1,
    )


def empty_state(batch_size, heads_local, row_count):
    return (
        jnp.full((batch_size, heads_local, GROUP, row_count), masked_score, jnp.float32),
        jnp.zeros((batch_size, heads_local, GROUP, row_count), jnp.float32),
        jnp.zeros((batch_size, heads_local, GROUP, row_count, HD), jnp.float32),
    )


def softmax_update(running, queries, key_rows, val_rows, allowed, score_scale):
    highest, totals, mixed = running
    scores = (
        jnp.einsum("brkgd,bnkd->bkgrn", queries, key_rows, preferred_element_type=jnp.float32)
        * score_scale
    )
    scores = jnp.where(allowed, scores, masked_score)
    raised = jnp.maximum(highest, jnp.max(scores, axis=-1))
    weights = jnp.where(allowed, jnp.exp(scores - raised[..., None]), 0.0)
    totals = jnp.sum(weights, axis=-1)
    mixed = jnp.einsum(
        "bkgrn,bnkd->bkgrd",
        weights.astype(jnp.bfloat16),
        val_rows,
        preferred_element_type=jnp.float32,
    )
    return (raised, totals, mixed)


def normalize_rows(running):
    mixed = running[2] / running[1][..., None]
    batch_size, heads_local, group_size, row_count, head_dim = mixed.shape
    return (
        jnp.transpose(mixed, (0, 3, 1, 2, 4))
        .reshape(batch_size, row_count, heads_local * group_size * head_dim)
        .astype(jnp.bfloat16)
    )


def decode_rows(queries, segment_kv, cache_kv, fresh_kv, lengths, score_scale):
    slot_index = jnp.arange(cache_kv.shape[1], dtype=jnp.int32)
    step_index = jnp.arange(queries.shape[1], dtype=jnp.int32)
    segment_scores = (
        jnp.einsum(
            "sqkgd,ckd->sqkgc", queries, segment_kv[:, :, 0], preferred_element_type=jnp.float32
        )
        * score_scale
    )
    cache_scores = (
        jnp.einsum(
            "sqkgd,sjkd->sqkgj", queries, cache_kv[:, :, :, 0], preferred_element_type=jnp.float32
        )
        * score_scale
    )
    fresh_scores = (
        jnp.einsum(
            "sqkgd,stkd->sqkgt", queries, fresh_kv[:, :, :, 0], preferred_element_type=jnp.float32
        )
        * score_scale
    )
    cache_allowed = (slot_index[None, :] < lengths[:, None])[:, None, None, None, :]
    fresh_allowed = (step_index[None, :] <= step_index[:, None])[None, :, None, None, :]
    cache_scores = jnp.where(cache_allowed, cache_scores, masked_score)
    fresh_scores = jnp.where(fresh_allowed, fresh_scores, masked_score)
    highest = jnp.maximum(
        jnp.maximum(jnp.max(segment_scores, axis=-1), jnp.max(cache_scores, axis=-1)),
        jnp.max(fresh_scores, axis=-1),
    )[..., None]
    segment_weights = jnp.exp(segment_scores - highest)
    cache_weights = jnp.where(cache_allowed, jnp.exp(cache_scores - highest), 0.0)
    fresh_weights = jnp.where(fresh_allowed, jnp.exp(fresh_scores - highest), 0.0)
    totals = (
        jnp.sum(segment_weights, axis=-1)
        + jnp.sum(cache_weights, axis=-1)
        + jnp.sum(fresh_weights, axis=-1)
    )
    mixed = jnp.einsum(
        "sqkgc,ckd->sqkgd",
        segment_weights.astype(jnp.bfloat16),
        segment_kv[:, :, 1],
        preferred_element_type=jnp.float32,
    )
    mixed = mixed + jnp.einsum(
        "sqkgj,sjkd->sqkgd",
        cache_weights.astype(jnp.bfloat16),
        cache_kv[:, :, :, 1],
        preferred_element_type=jnp.float32,
    )
    mixed = mixed + jnp.einsum(
        "sqkgt,stkd->sqkgd",
        fresh_weights.astype(jnp.bfloat16),
        fresh_kv[:, :, :, 1],
        preferred_element_type=jnp.float32,
    )
    sample_count, step_count, heads_local, group_size, head_dim = mixed.shape
    return (
        (mixed / totals[..., None])
        .reshape(sample_count, step_count, heads_local * group_size * head_dim)
        .astype(jnp.bfloat16)
    )


def on_device(
    prefill_query,
    prefill_kv,
    decode_query,
    gen_cache,
    new_hidden,
    norm_gain,
    kv_weight,
    prompt_of,
    cached_len,
):
    score_scale = HD ** (-0.5)
    queries = prefill_query[0]
    keyvals = prefill_kv[0]
    prompts = queries.shape[0]
    tokens = queries.shape[1]
    heads_local = keyvals.shape[-1] // (2 * HD)
    pool_number = lax.axis_index("pd")
    own_row = lax.dynamic_index_in_dim(prompt_of, pool_number, 0, keepdims=False)
    grouped = queries.reshape(prompts, tokens, heads_local, GROUP, HD)
    query_pos = lax.axis_index("ctx") * tokens + jnp.arange(tokens, dtype=jnp.int32)
    block_rows = lax.all_gather(keyvals, "ctx", axis=1, tiled=True)
    key_count = block_rows.shape[1]
    parted = block_rows.reshape(prompts, key_count, heads_local, 2, HD)
    key_pos = jnp.arange(key_count, dtype=jnp.int32)
    allowed = key_pos[None, :] <= query_pos[:, None]
    running = softmax_update(
        empty_state(prompts, heads_local, tokens),
        grouped,
        parted[:, :, :, 0],
        parted[:, :, :, 1],
        allowed,
        score_scale,
    )
    segment_out = normalize_rows(running)
    sending = lax.all_to_all(
        jnp.take(keyvals, own_row, axis=0), "ctx", split_axis=0, concat_axis=1, tiled=True
    )[0]
    relayed = shifted(sending, "pd", 1)
    hidden = new_hidden[0, 0]
    samples = hidden.shape[0]
    steps = hidden.shape[1]
    wide = lax.all_gather(hidden, "tp", axis=2, tiled=True).astype(jnp.float32)
    scaled = (wide * norm_gain).astype(jnp.bfloat16)
    projected = jnp.einsum("sqn,nc->sqc", scaled, kv_weight, preferred_element_type=jnp.float32)
    projected, squares = (projected, jnp.sum(wide * wide, axis=-1))
    normed = (projected * lax.rsqrt(squares / D + 1e-06)[..., None]).reshape(
        samples, steps, heads_local, 2, HD
    )
    lengths = cached_len[0, 0]
    segment_length = relayed.shape[0]
    new_positions = (
        segment_length + lengths[:, None] + jnp.arange(steps, dtype=jnp.int32)[None, :]
    ).astype(jnp.float32)
    rotated = rotate_keys(normed[:, :, :, 0], new_positions[:, :, None])
    fresh_kv = jnp.stack([rotated, normed[:, :, :, 1]], axis=3).astype(jnp.bfloat16)
    step_query = decode_query[0, 0].reshape(samples, steps, heads_local, GROUP, HD)
    segment_rows = relayed.reshape(segment_length, heads_local, 2, HD)
    cache_rows = gen_cache[0, 0].reshape(samples, gen_cache.shape[3], heads_local, 2, HD)
    decode_out = decode_rows(step_query, segment_rows, cache_rows, fresh_kv, lengths, score_scale)
    return (segment_out[None], decode_out[None, None])


def solution(mesh):
    placed = (
        P("pd", None, "ctx", "tp"),
        P("pd", None, "ctx", "tp"),
        P("pd", "ctx", None, None, "tp"),
        P("pd", "ctx", None, None, "tp"),
        P("pd", "ctx", None, None, "tp"),
        P(),
        P(None, "tp"),
        P(),
        P("pd", "ctx", None),
    )
    return jax.shard_map(
        on_device,
        mesh=mesh,
        in_specs=placed,
        out_specs=(P("pd", None, "ctx", "tp"), P("pd", "ctx", None, None, "tp")),
        check_vma=False,
    )
```

profile of v0, /device:TPU:38, one launch (start us, length us, event | category | flops | bytes accessed | tf_op | source)
XLA Modules:
  0.0 302.0 jit_solution(10758247433639857722)
XLA Ops:
  7.2 0.7 all-gather.7.cloned.1.call-update
  7.9 0.7 fusion.75
  8.6 1.6 gather_fusion
  10.3 0.7 compare_and_fusion
  11.0 1.6 broadcast_select_fusion
  12.6 8.7 %all-to-all-start = ((bf16[16,256,256]{2,1,0:T(8,128)(2,1)}), bf16[16,256,256]{2,1,0:T(8,128)(2,1)S(1)}, u32[]{:S(2)}, u32[]{:S(2)}) async-start(bf16[16,256,256]{2,1,0:T(8,128)(2,1)} %broadcast_select_fusion), calls=%async_computation | async-start | bytes 4194304 | tf_op jit(solution)/shard_map/all_to_all | solution.py:172
  21.3 0.9 copy.95
  22.2 1.2 copy.142
  23.5 3.9 %copy.104 = bf16[1,1,16,256,256]{3,4,2,1,0:T(8,128)(2,1)} copy(bf16[1,1,16,256,256]{4,3,2,1,0:T(8,128)(2,1)} %param.12) | data formatting | bytes 4194304 | tf_op args[3]
  27.5 2.4 fusion.84
  30.1 104.1 %all-to-all-done = bf16[16,256,256]{2,1,0:T(8,128)(2,1)S(1)} async-done(((bf16[16,256,256]{2,1,0:T(8,128)(2,1)}), bf16[16,256,256]{2,1,0:T(8,128)(2,1)S(1)}, u32[]{:S(2)}, u32[]{:S(2)}) %all-to-all-start) | async-done | bytes 2097184 | tf_op jit(solution)/shard_map/all_to_all | solution.py:172
  134.2 2.9 copy.131
  137.1 4.5 %collective-permute-start = (bf16[4096,256]{0,1:T(8,128)(2,1)}, bf16[4096,256]{0,1:T(8,128)(2,1)}, u32[]{:S(2)}, u32[]{:S(2)}) collective-permute-start(bf16[4096,256]{0,1:T(8,128)(2,1)} %copy.131), channel_id=1, source_target_pairs={{1,0},{0,1},{3,2},{2,3},{5,4},{4,5},{7,6},{6,7},{9,8},{8,9},{11,10... | collective-permute-start | bytes 6291464 | tf_op jit(solution)/shard_map/ppermute | solution.py:17
  141.6 0.7 iota_compare_fusion
  142.3 2.3 fusion.16
  144.6 0.1 copy.108
  144.7 3.3 %fusion.31 = f32[16,4,256]{2,0,1:T(8,128)S(1)} fusion(bf16[8192,256]{1,0:T(8,128)(2,1)} %param.15, bf16[16,4,8192]{2,1,0:T(4,128)(2,1)S(1)} %get-tuple-element.13, f32[16,4]{0,1:T(4,128)S(1)} %add_rsqrt_fusion), kind=kOutput, calls=%fused_computation.37 | convolution fusion | flops 268451840 | bytes 5308672 | tf_op jit(solution)/shard_map/sqn,nc->sqc/dot_general | solution.py:181
  148.2 0.3 fusion.68
  148.5 0.7 fusion.83
  149.4 52.1 %collective-permute-done = bf16[4096,256]{0,1:T(8,128)(2,1)} collective-permute-done((bf16[4096,256]{0,1:T(8,128)(2,1)}, bf16[4096,256]{0,1:T(8,128)(2,1)}, u32[]{:S(2)}, u32[]{:S(2)}) %collective-permute-start) | collective-permute-done | bytes 2097184 | tf_op jit(solution)/shard_map/ppermute | solution.py:17
  201.5 5.7 %bitcast_reduce_fusion = (f32[16,4,8]{0,2,1:T(8,128)S(1)}, f32[4096,16,4,8]{0,1,3,2:T(8,128)}) fusion(bf16[16,4,8,128]{3,2,1,0:T(8,128)(2,1)S(1)} %reshape.347, bf16[4096,1,2,128]{0,3,2,1:T(8,128)(2,1)} %bitcast.18), kind=kOutput, calls=%fused_computation.10 | convolution fusion | flops 541064704 | bytes 9570304 | tf_op jit(solution)/shard_map/sqkgd,ckd->sqkgc/dot_general | solution.py:78
  207.2 0.2 fusion.55
  207.5 1.5 fusion.45
  209.1 5.0 %fusion.8 = f32[16,4,8]{0,2,1:T(8,128)S(1)} fusion(f32[4096,16,4,8]{0,1,3,2:T(8,128)} %get-tuple-element.21, f32[16,4,8]{0,2,1:T(8,128)S(1)} %maximum_maximum_fusion), kind=kLoop, calls=%fused_computation.12 | loop fusion | flops 6290944 | bytes 8392704 | tf_op jit(solution)/shard_map/reduce_sum | solution.py:107
  214.1 0.3 fusion.58
  214.4 1.5 fusion.41
  216.0 3.2 %fusion.38 = bf16[16,4,1,8,128]{4,0,3,1,2:T(8,128)(2,1)S(1)} fusion(f32[4096,16,4,8]{0,1,3,2:T(8,128)S(1)} %copy-done.1, f32[16,4,8]{0,2,1:T(8,128)S(1)} %maximum_maximum_fusion, bf16[4096,1,2,128]{0,3,2,1:T(8,128)(2,1)} %bitcast.18, f32[16,128,4,8]{1,3,2,0:T(8,128)S(1)} %fusion.58, f32[16,4,8,128]{3,2,1,0:T(8,128)S(1)} %fusion.41, ...), kind=kOutput, calls=%fused_computation.40 | convolution fusion | flops 543424512 | bytes 10096640 | tf_op jit(solution)/shard_map/sqkgc,ckd->sqkgd/dot_general | solution.py:111
  219.2 0.7 reshape.377
  219.9 26.5 %fusion = (f32[2,8,256]{2,1,0:T(8,128)S(1)}, f32[2,4096,256,8]{2,1,3,0:T(8,128)}) fusion(pred[256,4096]{0,1:T(8,128)(4,1)S(1)} %iota_compare_fusion, bf16[2,256,8,128]{3,2,1,0:T(8,128)(2,1)} %bitcast.221, bf16[2,4096,1,2,128]{1,4,3,0,2:T(8,128)(2,1)} %bitcast.225), kind=kOutput, calls=%fused_computation.3 | convolution fusion | flops 4345294848 | bytes 71319552 | tf_op jit(solution)/shard_map/brkgd,bnkd->bkgrn/dot_general | solution.py:48
  246.4 21.7 %fusion.1 = f32[2,8,256]{2,1,0:T(8,128)S(1)} fusion(f32[2,4096,256,8]{2,1,3,0:T(8,128)} %get-tuple-element.17, f32[2,8,256]{2,1,0:T(8,128)S(1)} %broadcast_maximum_fusion, pred[256,4096]{0,1:T(8,128)(4,1)S(1)} %iota_compare_fusion), kind=kLoop, calls=%fused_computation.4 | loop fusion | flops 83881984 | bytes 68190208 | tf_op jit(solution)/shard_map/reduce_sum | solution.py:54
  268.1 25.7 %divide_convert_fusion = bf16[2,8,256,128]{2,3,1,0:T(8,128)(2,1)S(1)} fusion(f32[2,8,256]{2,1,0:T(8,128)S(1)} %fusion.1, f32[2,4096,256,8]{2,1,3,0:T(8,128)} %get-tuple-element.17, f32[2,8,256]{2,1,0:T(8,128)S(1)} %broadcast_maximum_fusion, pred[256,4096]{0,1:T(8,128)(4,1)S(1)} %iota_compare_fusion, bf16[2,4096,1,2,128]{1,4,3,0,2:T(8,128)(2,1)} %bitcast.226), kind=kOutput, calls=%fused_computation.26 | convolution fusion | flops 4379901952 | bytes 71335936 | tf_op jit(solution)/shard_map/bkgrn,bnkd->bkgrd/dot_general | solution.py:55
  293.9 1.3 copy.120
  (41 shorter events, 0.9 us)
Async XLA Ops:
  7.2 14.1 %copy-start = (bf16[1,2,256,256]{3,2,1,0:T(8,128)(2,1)S(1)}, bf16[1,2,256,256]{3,2,1,0:T(8,128)(2,1)}, u32[]{:S(2)}) copy-start(bf16[1,2,256,256]{3,2,1,0:T(8,128)(2,1)} %param.10) | copy-start | bytes 786436
  7.2 15.0 %copy-start.3 = (bf16[1,2,256,1024]{3,2,1,0:T(8,128)(2,1)S(1)}, bf16[1,2,256,1024]{3,2,1,0:T(8,128)(2,1)}, u32[]{:S(2)}) copy-start(bf16[1,2,256,1024]{3,2,1,0:T(8,128)(2,1)} %param.9) | copy-start | bytes 3145732
  7.2 16.3 %copy-start.4 = (bf16[1,1,16,4,1024]{4,3,2,1,0:T(4,128)(2,1)S(1)}, bf16[1,1,16,4,1024]{4,3,2,1,0:T(4,128)(2,1)}, u32[]{:S(2)}) copy-start(bf16[1,1,16,4,1024]{4,3,2,1,0:T(4,128)(2,1)} %param.11) | copy-start | bytes 393220
  7.2 135.1 %all-gather.7.cloned.1.call-start = ((), (), s32[]{:S(2)}) async-start(), calls=%async_computation.2 | async-start | bytes 1179648 | tf_op jit(solution)/shard_map/all_gather | solution.py:179
  10.3 17.2 %copy-start.6 = (s32[1,1,16]{2,1,0:T(1,128)S(1)}, s32[1,1,16]{2,1,0:T(1,128)}, u32[]{:S(2)}) copy-start(s32[1,1,16]{2,1,0:T(1,128)} %param.17) | copy-start | bytes 196
  12.6 121.6 %all-to-all-start = ((bf16[16,256,256]{2,1,0:T(8,128)(2,1)}), bf16[16,256,256]{2,1,0:T(8,128)(2,1)S(1)}, u32[]{:S(2)}, u32[]{:S(2)}) async-start(bf16[16,256,256]{2,1,0:T(8,128)(2,1)} %broadcast_select_fusion), calls=%async_computation | async-start | bytes 4194304 | tf_op jit(solution)/shard_map/all_to_all | solution.py:172
  21.3 198.6 %all-gather.5.cloned.1.call-start = ((), (), s32[]{:S(2)}) async-start(), calls=%async_computation.1 | async-start | bytes 4456448 | tf_op jit(solution)/shard_map/all_gather | solution.py:158
  22.2 120.2 %copy-start.5 = (f32[8192]{0:T(1024)S(1)}, f32[8192]{0:T(1024)}, u32[]{:S(2)}) copy-start(f32[8192]{0:T(1024)} %param.14) | copy-start | bytes 98308
  137.1 64.4 %collective-permute-start = (bf16[4096,256]{0,1:T(8,128)(2,1)}, bf16[4096,256]{0,1:T(8,128)(2,1)}, u32[]{:S(2)}, u32[]{:S(2)}) collective-permute-start(bf16[4096,256]{0,1:T(8,128)(2,1)} %copy.131), channel_id=1, source_target_pairs={{1,0},{0,1},{3,2},{2,3},{5,4},{4,5},{7,6},{6,7},{9,8},{8,9},{11,10... | collective-permute-start | bytes 6291464 | tf_op jit(solution)/shard_map/ppermute | solution.py:17
  207.2 7.3 %copy-start.2 = (bf16[1,1,16,256,256]{3,4,2,1,0:T(8,128)(2,1)S(1)}, bf16[1,1,16,256,256]{3,4,2,1,0:T(8,128)(2,1)}, u32[]{:S(2)}) copy-start(bf16[1,1,16,256,256]{3,4,2,1,0:T(8,128)(2,1)} %copy.104) | copy-start | bytes 6291460
  209.1 6.9 %copy-start.1 = (f32[4096,16,4,8]{0,1,3,2:T(8,128)S(1)}, f32[4096,16,4,8]{0,1,3,2:T(8,128)}, u32[]{:S(2)}) copy-start(f32[4096,16,4,8]{0,1,3,2:T(8,128)} %get-tuple-element.21) | copy-start | bytes 25165828
Sparse Core Ops, SparseCore 0:
  9.9 26.8 all-gather.6
  38.5 176.3 all-gather.4
where the time goes:
time: 303 us; the launch traced here: 302 us
  waiting for transfers between devices  157 us (52%)
  matrix products  69.4 us (23%)
  other arithmetic  34.9 us (12%)
  between operations  14.3 us (5%)
  local copies, waits for them, and re-layouts  13.3 us (4%)
  starting transfers between devices  13.3 us (4%)
    all_to_all x1, waiting for transfers between devices, on_device(): lax.all_to_all(jnp.take(keyvals, own_row, axis=0), 'ctx', split_axis=0, c...  104 us
    ppermute x1, waiting for transfers between devices, shifted(): return lax.ppermute(block, axis, route)  52.1 us
    dot_general x1, matrix products, softmax_update(): jnp.einsum('brkgd,bnkd->bkgrn', queries, key_rows, preferred_element_type...  26.5 us
    dot_general x1, matrix products, softmax_update(): jnp.einsum('bkgrn,bnkd->bkgrd', weights.astype(jnp.bfloat16), val_rows, p...  25.7 us
    reduce_sum x1, other arithmetic, softmax_update(): totals = jnp.sum(weights, axis=-1)  21.7 us
    all_to_all x1, starting transfers between devices, on_device(): lax.all_to_all(jnp.take(keyvals, own_row, axis=0), 'ctx', split_axis=0, c...  8.65 us
    unnamed x21, local copies, waits for them, and re-layouts  8.12 us
  transfers between devices with their start and end apart: 4, of which 2 were waited for; matrix products, arithmetic and copies ran while one was open for 14% of the time, Pallas kernels for 0%

commit v1 on v0

v1 whole, which is shorter than its diff:
```python
import functools

import jax
import jax.numpy as jnp
from jax import lax
from jax.experimental import pallas as pl
from jax.experimental.pallas import tpu as pltpu
from jax.sharding import PartitionSpec as P

D = 8192
HD = 128
GROUP = 8
BLOCK = 256
MASKED = -1e30
LOG2E = 1.4426950408889634
SCALE2 = HD ** (-0.5) * LOG2E
VMEM_LIMIT = 40 * 1024 * 1024

bf16 = jnp.bfloat16
f32 = jnp.float32


def scores_of(rows, keys):
    return lax.dot_general(rows, keys, (((1,), (1,)), ((), ())), preferred_element_type=f32)


def fill_values(aug_ref, index, block):
    aug_ref[index, :, :HD] = block[:, HD:]
    aug_ref[index, :, HD:] = jnp.ones((BLOCK, HD), bf16)


def weigh(parts, highest, aug_blocks):
    out = None
    for part, aug in zip(parts, aug_blocks):
        weights = jnp.exp2((part - highest) * SCALE2).astype(bf16)
        term = jnp.dot(weights, aug, preferred_element_type=f32)
        out = term if out is None else out + term
    return out


def max_of(parts):
    top = parts[0]
    for part in parts[1:]:
        top = jnp.maximum(top, part)
    return jnp.max(top, axis=-1, keepdims=True)


def first_kernel(info, own_q, partner_q, *refs):
    blocks = refs[:8]
    acc_ref, stat_ref, q_scr, key_scr, aug_scr = refs[8:]
    parity, row_y = info[0], info[1]
    q_scr[0] = own_q[...]
    q_scr[1] = partner_q[...]
    for group in range(2):
        for b in range(4):
            block = blocks[group * 4 + b][...]
            key_scr[group * 4 + b] = block[:, :HD]
            fill_values(aug_scr, group * 4 + b, block)
    lane = lax.broadcasted_iota(jnp.int32, (BLOCK, HD), 1)
    upper = lax.broadcasted_iota(jnp.int32, (BLOCK, BLOCK), 1) > lax.broadcasted_iota(
        jnp.int32, (BLOCK, BLOCK), 0
    )

    def shift_of(b):
        block_y = (row_y + (0, 3, 1, 2)[b]) % 4
        return jnp.where(block_y < row_y, 0.0, MASKED).astype(f32)

    for odd in (True, False):
        side = 1 - parity if odd else parity
        same = side * 4
        other = (1 - side) * 4

        def head(h, carry):
            rows = q_scr[side, :, pl.ds(pl.multiple_of(h * HD, HD), HD)]
            parts = []
            augs = []
            for b in range(4):
                part = scores_of(rows, key_scr[same + b])
                if b == 0:
                    part = jnp.where(upper, MASKED, part)
                else:
                    part = part + shift_of(b)
                parts.append(part)
                augs.append(aug_scr[same + b])
            if odd:
                for b in range(4):
                    parts.append(scores_of(rows, key_scr[other + b]))
                    augs.append(aug_scr[other + b])
            highest = max_of(parts)
            mixed = weigh(parts, highest, augs)
            acc_ref[side, h] = mixed[:, :HD]
            old = jnp.where(lane == h, highest, stat_ref[side])
            stat_ref[side] = jnp.where(lane == h + 8, mixed[:, HD:], old)
            return carry

        lax.fori_loop(0, GROUP, head, 0)


def last_kernel(info, q_ref, acc_ref, stat_ref, *refs):
    kv_refs = refs[:4]
    out_ref, aug_scr = refs[4:]
    lane = lax.broadcasted_iota(jnp.int32, (BLOCK, HD), 1)

    def column(h):
        return jnp.sum(jnp.where(lane == h, stat_ref[0], 0.0), axis=-1, keepdims=True)

    @pl.when(info[2] >= 2)
    def _():
        for b in range(8):
            fill_values(aug_scr, b, kv_refs[b // 2][b % 2])

        def head(h, carry):
            at = pl.ds(pl.multiple_of(h * HD, HD), HD)
            rows = q_ref[:, at]
            parts = [scores_of(rows, kv_refs[b // 2][b % 2, :, :HD]) for b in range(8)]
            before = column(h)
            highest = jnp.maximum(before, max_of(parts))
            mixed = weigh(parts, highest, [aug_scr[b] for b in range(8)])
            fade = jnp.exp2((before - highest) * SCALE2)
            total = column(h + 8) * fade + mixed[:, HD:]
            out_ref[:, at] = ((acc_ref[0, h] * fade + mixed[:, :HD]) / total).astype(bf16)
            return carry

        lax.fori_loop(0, GROUP, head, 0)

    @pl.when(info[2] < 2)
    def _():
        def head(h, carry):
            at = pl.ds(pl.multiple_of(h * HD, HD), HD)
            out_ref[:, at] = (acc_ref[0, h] / column(h + 8)).astype(bf16)
            return carry

        lax.fori_loop(0, GROUP, head, 0)


def segment_kernel(info, q0_ref, q1_ref, *refs):
    near = refs[:8]
    far = refs[8:12]
    out0_ref, out1_ref, aug_scr = refs[12:]

    def keys(b):
        if b < 8:
            return near[b][:, :HD]
        return far[(b - 8) // 2][(b - 8) % 2, :, :HD]

    for b in range(16):
        block = near[b][...] if b < 8 else far[(b - 8) // 2][(b - 8) % 2]
        fill_values(aug_scr, b, block)
    for which, (q_ref, out_ref) in enumerate(((q0_ref, out0_ref), (q1_ref, out1_ref))):

        @pl.when(info[3 + which] == 1)
        def _():
            pieces = []
            for tile in range(2):
                rows = q_ref[tile * 256 : tile * 256 + 256]
                parts = [scores_of(rows, keys(b)) for b in range(16)]
                highest = max_of(parts)
                mixed = weigh(parts, highest, [aug_scr[b] for b in range(16)])
                total = mixed[:, HD:]
                out_ref[tile * 256 : tile * 256 + 256] = (mixed[:, :HD] / total).astype(bf16)
                level = highest * SCALE2 + jnp.log2(total)
                turned = jnp.transpose(level)[0:1]
                pieces += [turned[:, :128], turned[:, 128:]]
            level = jnp.concatenate(pieces, axis=0)
            high = level.astype(bf16)
            rest = level - high.astype(f32)
            middle = rest.astype(bf16)
            low = (rest - middle.astype(f32)).astype(bf16)
            out_ref[512:528] = jnp.concatenate(
                [high.astype(f32), middle.astype(f32), low.astype(f32), jnp.zeros((4, HD), f32)],
                axis=0,
            ).astype(bf16)

        @pl.when(info[3 + which] != 1)
        def _():
            out_ref[...] = jnp.zeros_like(out_ref)


def local_kernel(
    len_ref, hidden_ref, gain_ref, weight_ref, cos_ref, sin_ref, q_ref, cache_ref, out_ref, level_ref
):
    width = hidden_ref.shape[2]
    squares = jnp.zeros((64, 1), f32)
    projected = jnp.zeros((64, 2 * HD), f32)
    for part in range(D // width):
        wide = hidden_ref[part].astype(f32)
        squares = squares + jnp.sum(wide * wide, axis=-1, keepdims=True)
        scaled = (wide * gain_ref[:, part * width : (part + 1) * width]).astype(bf16)
        projected = projected + jnp.dot(
            scaled, weight_ref[part * width : (part + 1) * width], preferred_element_type=f32
        )
    normed = projected * lax.rsqrt(squares / D + 1e-6)
    key_rows = normed[:, :HD]
    turned = jnp.concatenate([key_rows[:, HD // 2 :], key_rows[:, : HD // 2]], axis=1)
    fresh_k = (key_rows * cos_ref[...] + turned * sin_ref[...]).astype(bf16)
    fresh_v = normed[:, HD:].astype(bf16)
    fresh_aug = jnp.concatenate([fresh_v, jnp.ones((64, HD), bf16)], axis=1)
    ones = jnp.ones((BLOCK, HD), bf16)
    slot = lax.broadcasted_iota(jnp.int32, (32, BLOCK), 1)
    fresh_slot = lax.broadcasted_iota(jnp.int32, (32, 64), 1)
    step = lax.broadcasted_iota(jnp.int32, (32, 64), 0) // GROUP

    for s in range(16):
        rows = q_ref[s * 32 : (s + 1) * 32]
        cache_part = jnp.where(
            slot < len_ref[s], scores_of(rows, cache_ref[s, :, :HD]), MASKED
        )
        allowed = (fresh_slot >= s * 4) & (fresh_slot <= s * 4 + step)
        fresh_part = jnp.where(allowed, scores_of(rows, fresh_k), MASKED)
        highest = jnp.maximum(
            jnp.max(cache_part, axis=-1, keepdims=True), jnp.max(fresh_part, axis=-1, keepdims=True)
        )
        cache_aug = jnp.concatenate([cache_ref[s, :, HD:], ones], axis=1)
        mixed = weigh([cache_part, fresh_part], highest, [cache_aug, fresh_aug])
        total = mixed[:, HD:]
        out_ref[s * 32 : (s + 1) * 32] = mixed[:, :HD] / total
        level_ref[s * 32 : (s + 1) * 32] = highest * SCALE2 + jnp.log2(total)


def merge_kernel(info, local_ref, level_ref, same_ref, other_ref, out_ref):
    def merge(part_ref):
        stat = part_ref[512:528].astype(f32)
        level = stat[0:4] + stat[4:8] + stat[8:12]
        for tile in range(4):
            at = slice(tile * 128, tile * 128 + 128)
            far = jnp.transpose(jnp.broadcast_to(level[tile : tile + 1], (128, 128)))
            near = level_ref[at]
            top = jnp.maximum(far, near)
            far_share = jnp.exp2(far - top)
            near_share = jnp.exp2(near - top)
            mixed = part_ref[at].astype(f32) * far_share + local_ref[at] * near_share
            out_ref[at] = (mixed / (far_share + near_share)).astype(bf16)

    @pl.when(info[5] == 1)
    def _():
        merge(same_ref)

    @pl.when(info[5] != 1)
    def _():
        merge(other_ref)


SMEM = pl.BlockSpec(memory_space=pltpu.SMEM)
VMEM = pl.BlockSpec(memory_space=pltpu.VMEM)


def call(kernel, out_shape, args, scalars=1, scratch=(), flops=0, touched=0, exps=0, specs=None):
    in_specs = [SMEM] * scalars + [VMEM] * (len(args) - scalars)
    for place, spec in (specs or {}).items():
        in_specs[place] = spec
    return pl.pallas_call(
        kernel,
        grid=(1,) if specs else (),
        out_shape=out_shape,
        in_specs=in_specs,
        out_specs=jax.tree.map(lambda _: VMEM, out_shape),
        scratch_shapes=list(scratch),
        compiler_params=pltpu.CompilerParams(vmem_limit_bytes=VMEM_LIMIT),
        cost_estimate=pl.CostEstimate(flops=flops, bytes_accessed=touched, transcendentals=exps),
    )(*args)


def y_turn(block, distance):
    route = [(i, i // 4 * 4 + (i % 4 + distance) % 4) for i in range(16)]
    return lax.ppermute(block, "ctx", route)


def z_swap(block, bits):
    return lax.ppermute(block, "ctx", [(i, i ^ (4 * bits)) for i in range(16)])


def y_all(block):
    return [block, y_turn(block, 1), y_turn(block, -1), y_turn(block, 2)]


def pool_swap(block, z_bits):
    route = [(i, (i ^ 1) ^ (8 * z_bits)) for i in range(32)]
    return lax.ppermute(block, ("ctx", "pd"), route)


def on_device(
    prefill_query,
    prefill_kv,
    decode_query,
    gen_cache,
    new_hidden,
    norm_gain,
    kv_weight,
    prompt_of,
    cached_len,
):
    queries = prefill_query[0]
    keyvals = prefill_kv[0]
    place = lax.axis_index("ctx")
    pool = lax.axis_index("pd")
    z, y = place // 4, place % 4
    parity = z % 2
    here = lax.dynamic_index_in_dim(prompt_of, pool, 0, keepdims=False)
    there = lax.dynamic_index_in_dim(prompt_of, 1 - pool, 0, keepdims=False)
    info = jnp.stack(
        [
            parity,
            y,
            z,
            (here[place] == parity).astype(jnp.int32),
            (here[place ^ 4] == parity).astype(jnp.int32),
            (there[place] == parity).astype(jnp.int32),
        ]
    ).astype(jnp.int32)

    even = parity == 0
    kv_keep = jnp.where(even, keyvals[0], keyvals[1])
    kv_give = jnp.where(even, keyvals[1], keyvals[0])
    from_z1 = z_swap(kv_give, 1)
    from_z2 = z_swap(kv_keep, 2)
    from_z3 = z_swap(kv_give, 3)
    group0 = y_all(kv_keep)
    q_keep = jnp.where(even, queries[0], queries[1])
    q_give = jnp.where(even, queries[1], queries[0])
    q_partner = z_swap(q_give, 1)
    group1 = y_all(from_z1)
    group23 = y_all(jnp.stack([from_z2, from_z3]))

    hidden = new_hidden[0, 0]
    samples, steps, width = hidden.shape
    wide = lax.all_gather(hidden.reshape(samples * steps, width), "tp", axis=0)
    step_rows = decode_query[0, 0].reshape(samples * steps * GROUP, HD)
    rows0 = pool_swap(step_rows, 0)
    rows1 = pool_swap(step_rows, 1)

    lengths = cached_len[0, 0]
    half = HD // 2
    frequency = 1000000.0 ** (-jnp.arange(half, dtype=f32) * 2.0 / HD)
    positions = (4096 + lengths[:, None] + jnp.arange(steps, dtype=jnp.int32)[None, :]).astype(f32)
    angles = positions.reshape(-1)[:, None] * frequency
    cosine, sine = jnp.cos(angles), jnp.sin(angles)
    cos_all = jnp.concatenate([cosine, cosine], axis=-1)
    sin_all = jnp.concatenate([-sine, sine], axis=-1)

    shape = jax.ShapeDtypeStruct
    rows = samples * steps * GROUP
    local_out, local_level = call(
        local_kernel,
        (shape((rows, HD), f32), shape((rows, HD), f32)),
        (
            lengths,
            wide,
            norm_gain[None],
            kv_weight,
            cos_all,
            sin_all,
            step_rows,
            gen_cache[0, 0],
        ),
        flops=2 * 64 * D * 256,
        touched=8 << 20,
        exps=rows * 320,
    )

    acc, stat = call(
        first_kernel,
        (shape((2, GROUP, BLOCK, HD), f32), shape((2, BLOCK, HD), f32)),
        (info, q_keep, q_partner, *group0, *group1),
        scratch=(
            pltpu.VMEM((2, BLOCK, GROUP * HD), bf16),
            pltpu.VMEM((8, BLOCK, HD), bf16),
            pltpu.VMEM((8, BLOCK, 2 * HD), bf16),
        ),
        flops=3 * 2048 * 1024 * 512,
        touched=4 << 20,
        exps=3 * 2048 * 1024,
    )
    segment0, segment1 = call(
        segment_kernel,
        (shape((rows + 16, HD), bf16), shape((rows + 16, HD), bf16)),
        (info, rows0, rows1, *group0, *group1, *group23),
        scratch=(pltpu.VMEM((16, BLOCK, 2 * HD), bf16),),
        flops=1024 * 4096 * 512,
        touched=3 << 20,
        exps=1024 * 4096,
    )
    back0 = pool_swap(segment0, 0)
    back1 = pool_swap(segment1, 1)

    def finish(q_rows, side):
        return call(
            last_kernel,
            shape((BLOCK, GROUP * HD), bf16),
            (info, q_rows, acc, stat, *group23),
            scratch=(pltpu.VMEM((8, BLOCK, 2 * HD), bf16),),
            flops=2 * 2048 * 1024 * 512,
            touched=4 << 20,
            exps=2 * 2048 * 1024,
            specs={
                2: pl.BlockSpec((1, GROUP, BLOCK, HD), lambda i: (side, 0, 0, 0)),
                3: pl.BlockSpec((1, BLOCK, HD), lambda i: (side, 0, 0)),
            },
        )

    out_partner = finish(q_partner, 1)
    returned = z_swap(out_partner, 1)
    out_own = finish(q_keep, 0)
    merged = call(
        merge_kernel,
        shape((rows, HD), bf16),
        (info, local_out, local_level, back0, back1),
        flops=rows * HD * 8,
        touched=1 << 20,
        exps=rows * HD * 2,
    )
    decode_out = merged.reshape(samples, steps, GROUP * HD)
    segment_out = jnp.where(
        even, jnp.stack([out_own, returned]), jnp.stack([returned, out_own])
    )
    return (segment_out[None], decode_out[None, None])


def solution(mesh):
    placed = (
        P("pd", None, "ctx", "tp"),
        P("pd", None, "ctx", "tp"),
        P("pd", "ctx", None, None, "tp"),
        P("pd", "ctx", None, None, "tp"),
        P("pd", "ctx", None, None, "tp"),
        P(),
        P(None, "tp"),
        P(),
        P("pd", "ctx", None),
    )
    return jax.shard_map(
        on_device,
        mesh=mesh,
        in_specs=placed,
        out_specs=(P("pd", None, "ctx", "tp"), P("pd", "ctx", None, None, "tp")),
        check_vma=False,
    )
```

time: 303 us -> 120 us (0.40)
  the two profiles are of different devices: /device:TPU:38 before, /device:TPU:70 now
where the time goes in v1:
time: 120 us
  Pallas kernels  50.4 us (42%)
  starting transfers between devices  40.3 us (34%)
  between operations  16.3 us (14%)
  local copies, waits for them, and re-layouts  7.43 us (6%)
  other arithmetic  4.58 us (4%)
    pallas_call x6, Pallas kernels, call(): pl.pallas_call(kernel, grid=(1,) if specs else (), out_shape=out_shape, i...  50.4 us
    ppermute x4, starting transfers between devices, pool_swap(): return lax.ppermute(block, ('ctx', 'pd'), route)  16.7 us
    ppermute x9, starting transfers between devices, y_turn(): return lax.ppermute(block, 'ctx', route)  15.3 us
    ppermute x5, starting transfers between devices, z_swap(): return lax.ppermute(block, 'ctx', [(i, i ^ 4 * bits) for i in range(16)])  8.37 us
    unnamed x18, local copies, waits for them, and re-layouts  4.25 us
  transfers between devices with their start and end apart: 19, of which 1 were waited for; matrix products, arithmetic and copies ran while one was open for 5% of the time, Pallas kernels for 41%

profile of v1, /device:TPU:70, one launch (start us, length us, event | category | flops | bytes accessed | tf_op | source)
XLA Modules:
  0.0 119.9 jit_solution(2495385764744200460)
XLA Ops:
  7.3 1.0 select_bitcast_fusion.2
  8.5 1.9 %collective-permute-start.4 = (bf16[256,256]{1,0:T(8,128)(2,1)S(1)}, bf16[256,256]{1,0:T(8,128)(2,1)S(1)}, u32[]{:S(2)}, u32[]{:S(2)}) collective-permute-start(bf16[256,256]{1,0:T(8,128)(2,1)S(1)} %get-tuple-element.16), channel_id=1, source_target_pairs={{0,64},{16,80},{32,96},{48,112},{64,0},{80,16},{96,32},{112,48},{1... | collective-permute-start | bytes 393224 | tf_op jit(solution)/shard_map/ppermute | solution.py:269
  10.4 2.3 %collective-permute-start.8 = (bf16[256,256]{1,0:T(8,128)(2,1)S(1)}, bf16[256,256]{1,0:T(8,128)(2,1)S(1)}, u32[]{:S(2)}, u32[]{:S(2)}) collective-permute-start(bf16[256,256]{1,0:T(8,128)(2,1)S(1)} %get-tuple-element.17.refs_0_), channel_id=1, source_target_pairs={{0,128},{16,144},{32,160},{48,176},{64,192},{80,208},{96,224},{112... | collective-permute-start | bytes 393224 | tf_op jit(solution)/shard_map/ppermute | solution.py:269
  12.6 3.2 %collective-permute-start.3 = (bf16[256,256]{1,0:T(8,128)(2,1)S(1)}, bf16[256,256]{1,0:T(8,128)(2,1)S(1)}, u32[]{:S(2)}, u32[]{:S(2)}) collective-permute-start(bf16[256,256]{1,0:T(8,128)(2,1)S(1)} %get-tuple-element.17.refs_0_), channel_id=1, source_target_pairs={{0,32},{16,48},{32,0},{48,16},{64,96},{80,112},{96,64},{112,80},{1... | collective-permute-start | bytes 393224 | tf_op jit(solution)/shard_map/ppermute | solution.py:265
  15.8 1.6 %all_gather_reshape_squeeze.3 = bf16[1,64,1024]{2,1,0:T(8,128)(2,1)} reshape(bf16[1,1,16,4,1024]{4,3,2,1,0:T(4,128)(2,1)} %param.13) | data formatting | bytes 262144 | tf_op jit(solution)/shard_map/all_gather;reshape;squeeze | solution.py:326
  17.5 2.1 %select_bitcast_fusion.1 = (bf16[256,1024]{1,0:T(8,128)(2,1)S(1)}, bf16[256,1024]{1,0:T(8,128)(2,1)}) fusion(pred[]{:T(512)S(6)} %eq.15, bf16[1,2,256,1024]{3,2,1,0:T(8,128)(2,1)} %param.9), kind=kLoop, calls=%fused_computation.2 | loop fusion | flops 524288 | bytes 2097153 | tf_op jit(solution)/shard_map/jit(_where)/select_n | solution.py:318
  19.5 2.0 %collective-permute-start = (bf16[256,1024]{1,0:T(8,128)(2,1)}, bf16[256,1024]{1,0:T(8,128)(2,1)S(1)}, u32[]{:S(2)}, u32[]{:S(2)}) collective-permute-start(bf16[256,1024]{1,0:T(8,128)(2,1)} %get-tuple-element.15), channel_id=1, source_target_pairs={{0,64},{16,80},{32,96},{48,112},{64,0},{80,16},{96,32},{112,48},{1... | collective-permute-start | bytes 1572872 | tf_op jit(solution)/shard_map/ppermute | solution.py:269
  21.6 1.1 collective-permute-start.2
  22.8 1.0 collective-permute-start.1
  23.8 2.1 %collective-permute-start.7 = (bf16[256,256]{1,0:T(8,128)(2,1)S(1)}, bf16[256,256]{1,0:T(8,128)(2,1)S(1)}, u32[]{:S(2)}, u32[]{:S(2)}) collective-permute-start(bf16[256,256]{1,0:T(8,128)(2,1)S(1)} %collective-permute-done.4.refs_4_), channel_id=1, source_target_pairs={{0,32},{16,48},{32,0},{48,16},{64,96},{80,112},{96,64},{112,80},{1... | collective-permute-start | bytes 393224 | tf_op jit(solution)/shard_map/ppermute | solution.py:265
  25.8 1.3 %collective-permute-start.6 = (bf16[256,256]{1,0:T(8,128)(2,1)S(1)}, bf16[256,256]{1,0:T(8,128)(2,1)S(1)}, u32[]{:S(2)}, u32[]{:S(2)}) collective-permute-start(bf16[256,256]{1,0:T(8,128)(2,1)S(1)} %collective-permute-done.4.refs_4_), channel_id=1, source_target_pairs={{0,48},{16,0},{32,16},{48,32},{64,112},{80,64},{96,80},{112,96},{1... | collective-permute-start | bytes 393224 | tf_op jit(solution)/shard_map/ppermute | solution.py:265
  27.1 0.8 collective-permute-done.2.refs_2_
  27.9 1.5 %collective-permute-start.5 = (bf16[256,256]{1,0:T(8,128)(2,1)S(1)}, bf16[256,256]{1,0:T(8,128)(2,1)S(1)}, u32[]{:S(2)}, u32[]{:S(2)}) collective-permute-start(bf16[256,256]{1,0:T(8,128)(2,1)S(1)} %collective-permute-done.4.refs_4_), channel_id=1, source_target_pairs={{0,16},{16,32},{32,48},{48,0},{64,80},{80,96},{96,112},{112,64},{1... | collective-permute-start | bytes 393224 | tf_op jit(solution)/shard_map/ppermute | solution.py:265
  29.4 0.7 fusion.1
  32.3 3.5 %collective-permute-start.15 = (bf16[512,128]{1,0:T(8,128)(2,1)S(1)}, bf16[512,128]{1,0:T(8,128)(2,1)S(1)}, u32[]{:S(2)}, u32[]{:S(2)}) collective-permute-start(bf16[512,128]{1,0:T(8,128)(2,1)S(1)} %reshape_squeeze.3.q_ref), channel_id=1, source_target_pairs={{0,65},{1,64},{16,81},{17,80},{32,97},{33,96},{48,113},{49,112},{6... | collective-permute-start | bytes 393224 | tf_op jit(solution)/shard_map/ppermute | solution.py:278
  35.8 1.1 collective-permute-start.14
  36.9 3.1 %collective-permute-start.12 = (bf16[2,256,256]{2,1,0:T(8,128)(2,1)S(1)}, bf16[2,256,256]{2,1,0:T(8,128)(2,1)S(1)}, u32[]{:S(2)}, u32[]{:S(2)}) collective-permute-start(bf16[2,256,256]{2,1,0:T(8,128)(2,1)S(1)} %pad_maximum_fusion.refs_0_.refs_8_), channel_id=1, source_target_pairs={{0,32},{16,48},{32,0},{48,16},{64,96},{80,112},{96,64},{112,80},{1... | collective-permute-start | bytes 786440 | tf_op jit(solution)/shard_map/ppermute | solution.py:265
  40.0 2.0 %collective-permute-start.10 = (bf16[2,256,256]{2,1,0:T(8,128)(2,1)S(1)}, bf16[2,256,256]{2,1,0:T(8,128)(2,1)S(1)}, u32[]{:S(2)}, u32[]{:S(2)}) collective-permute-start(bf16[2,256,256]{2,1,0:T(8,128)(2,1)S(1)} %pad_maximum_fusion.refs_0_.refs_8_), channel_id=1, source_target_pairs={{0,16},{16,32},{32,48},{48,0},{64,80},{80,96},{96,112},{112,64},{1... | collective-permute-start | bytes 786440 | tf_op jit(solution)/shard_map/ppermute | solution.py:265
  42.0 18.5 %shard_map.104 = (f32[2,8,256,128]{3,2,1,0:T(8,128)S(1)}, f32[2,256,128]{2,1,0:T(8,128)S(1)}) custom-call(s32[6]{0:T(128)S(1)} %stack.62.info, bf16[256,1024]{1,0:T(8,128)(2,1)S(1)} %get-tuple-element.14.own_q.q_ref, bf16[256,1024]{1,0:T(8,128)(2,1)S(1)} %collective-permute-done.partner_q.q_ref, bf16[256,256]{1,0:T(8,128)(2,1)S(1)} %get-tuple-element.17.refs_0_, ...), custom_call_target="tpu_custom_call" | custom-call | flops 3221225472 | bytes 4194304 | tf_op jit(solution)/shard_map/pallas_call | solution.py:251
  60.6 11.8 %shard_map.106 = bf16[256,1024]{1,0:T(8,128)(2,1)S(1)} custom-call(s32[6]{0:T(128)S(1)} %stack.62.info, bf16[256,1024]{1,0:T(8,128)(2,1)S(1)} %collective-permute-done.partner_q.q_ref, f32[2,8,256,128]{3,2,1,0:T(8,128)S(1)} %get-tuple-element.8.acc_ref, f32[2,256,128]{2,1,0:T(8,128)S(1)} %get-tuple-element.9.stat_ref, ...), custom_call_target="tpu_custom_call" | custom-call | flops 2147483648 | bytes 4194304 | tf_op jit(solution)/shard_map/pallas_call | solution.py:251
  72.4 2.0 %collective-permute-start.13 = (bf16[256,1024]{1,0:T(8,128)(2,1)S(1)}, bf16[256,1024]{1,0:T(8,128)(2,1)S(1)}, u32[]{:S(2)}, u32[]{:S(2)}) collective-permute-start(bf16[256,1024]{1,0:T(8,128)(2,1)S(1)} %shard_map.106), channel_id=1, source_target_pairs={{0,64},{16,80},{32,96},{48,112},{64,0},{80,16},{96,32},{112,48},{1... | collective-permute-start | bytes 1572872 | tf_op jit(solution)/shard_map/ppermute | solution.py:269
  74.8 0.9 shard_map.108
  75.7 8.3 %collective-permute-start.16 = (bf16[528,128]{1,0:T(8,128)(2,1)S(1)}, bf16[528,128]{1,0:T(8,128)(2,1)S(1)}, u32[]{:S(2)}, u32[]{:S(2)}) collective-permute-start(bf16[528,128]{1,0:T(8,128)(2,1)S(1)} %get-tuple-element.12), channel_id=1, source_target_pairs={{0,1},{1,0},{16,17},{17,16},{32,33},{33,32},{48,49},{49,48},{64,65... | collective-permute-start | bytes 405512 | tf_op jit(solution)/shard_map/ppermute | solution.py:278
  84.0 3.8 %collective-permute-start.17 = (bf16[528,128]{1,0:T(8,128)(2,1)S(1)}, bf16[528,128]{1,0:T(8,128)(2,1)S(1)}, u32[]{:S(2)}, u32[]{:S(2)}) collective-permute-start(bf16[528,128]{1,0:T(8,128)(2,1)S(1)} %get-tuple-element.13), channel_id=1, source_target_pairs={{0,65},{1,64},{16,81},{17,80},{32,97},{33,96},{48,113},{49,112},{6... | collective-permute-start | bytes 405512 | tf_op jit(solution)/shard_map/ppermute | solution.py:278
  87.8 11.8 %shard_map.105 = bf16[256,1024]{1,0:T(8,128)(2,1)S(1)} custom-call(s32[6]{0:T(128)S(1)} %stack.62.info, bf16[256,1024]{1,0:T(8,128)(2,1)S(1)} %get-tuple-element.14.own_q.q_ref, f32[2,8,256,128]{3,2,1,0:T(8,128)S(1)} %get-tuple-element.8.acc_ref, f32[2,256,128]{2,1,0:T(8,128)S(1)} %get-tuple-element.9.stat_ref, ...), custom_call_target="tpu_custom_call" | custom-call | flops 2147483648 | bytes 4194304 | tf_op jit(solution)/shard_map/pallas_call | solution.py:251
  99.7 1.1 maximum_select_fusion
  100.8 0.8 copy-done.1
  101.6 2.2 %copy-done = bf16[8192,256]{1,0:T(8,128)(2,1)S(1)} copy-done((bf16[8192,256]{1,0:T(8,128)(2,1)S(1)}, bf16[8192,256]{1,0:T(8,128)(2,1)}, u32[]{:S(2)}) %copy-start) | copy-done | bytes 4194328
  103.8 1.2 %copy-done.2 = bf16[8,64,1024]{2,1,0:T(8,128)(2,1)S(1)} copy-done((bf16[8,64,1024]{2,1,0:T(8,128)(2,1)S(1)}, bf16[8,64,1024]{2,1,0:T(8,128)(2,1)}, u32[]{:S(2)}) %copy-start.2) | copy-done | bytes 1048600
  105.0 6.5 %shard_map.107 = (f32[512,128]{1,0:T(8,128)S(1)}, f32[512,128]{1,0:T(8,128)S(1)}) custom-call(s32[16]{0:T(128)S(1)} %bitcast.28, bf16[8,64,1024]{2,1,0:T(8,128)(2,1)S(1)} %copy-done.2, f32[1,8192]{1,0:T(1,128)S(1)} %bitcast.27, bf16[8192,256]{1,0:T(8,128)(2,1)S(1)} %copy-done, f32[64,128]{1,0:T(8,128)S(1)} %get-tuple-element.24.cos_ref, ...), custom_call_target="tpu_custom_call" | custom-call | flops 268435456 | bytes 8388608 | tf_op jit(solution)/shard_map/pallas_call | solution.py:251
  111.6 0.7 shard_map.109
  112.3 0.7 broadcast_in_dim_reshape.4
  (46 shorter events, 0.9 us)
Async XLA Ops:
  7.2 14.4 %copy-start.4 = (s32[1,1,16]{2,1,0:T(1,128)S(1)}, s32[1,1,16]{2,1,0:T(1,128)}, u32[]{:S(2)}) copy-start(s32[1,1,16]{2,1,0:T(1,128)} %param.17) | copy-start | bytes 196
  7.2 22.2 %copy-start.8 = (s32[2,16]{1,0:T(2,128)S(1)}, s32[2,16]{1,0:T(2,128)}, u32[]{:S(2)}) copy-start(s32[2,16]{1,0:T(2,128)} %param.16) | copy-start | bytes 388
  7.2 24.9 %copy-start.7 = (bf16[1,1,16,4,1024]{4,3,2,1,0:T(4,128)(2,1)S(1)}, bf16[1,1,16,4,1024]{4,3,2,1,0:T(4,128)(2,1)}, u32[]{:S(2)}) copy-start(bf16[1,1,16,4,1024]{4,3,2,1,0:T(4,128)(2,1)} %param.11) | copy-start | bytes 393220
  7.2 93.6 %all-gather.2.cloned.1.call-start = ((), (), s32[]{:S(2)}) async-start(), calls=%async_computation | async-start | bytes 1179648 | tf_op jit(solution)/shard_map/all_gather | solution.py:326
  8.3 13.3 %collective-permute-start.9 = (bf16[256,256]{1,0:T(8,128)(2,1)S(1)}, bf16[256,256]{1,0:T(8,128)(2,1)S(1)}, u32[]{:S(2)}, u32[]{:S(2)}) collective-permute-start(bf16[256,256]{1,0:T(8,128)(2,1)S(1)} %get-tuple-element.16), channel_id=1, source_target_pairs={{0,192},{16,208},{32,224},{48,240},{64,128},{80,144},{96,160},{112... | collective-permute-start | bytes 393224 | tf_op jit(solution)/shard_map/ppermute | solution.py:269
  8.5 14.3 %collective-permute-start.4 = (bf16[256,256]{1,0:T(8,128)(2,1)S(1)}, bf16[256,256]{1,0:T(8,128)(2,1)S(1)}, u32[]{:S(2)}, u32[]{:S(2)}) collective-permute-start(bf16[256,256]{1,0:T(8,128)(2,1)S(1)} %get-tuple-element.16), channel_id=1, source_target_pairs={{0,64},{16,80},{32,96},{48,112},{64,0},{80,16},{96,32},{112,48},{1... | collective-permute-start | bytes 393224 | tf_op jit(solution)/shard_map/ppermute | solution.py:269
  10.4 13.4 %collective-permute-start.8 = (bf16[256,256]{1,0:T(8,128)(2,1)S(1)}, bf16[256,256]{1,0:T(8,128)(2,1)S(1)}, u32[]{:S(2)}, u32[]{:S(2)}) collective-permute-start(bf16[256,256]{1,0:T(8,128)(2,1)S(1)} %get-tuple-element.17.refs_0_), channel_id=1, source_target_pairs={{0,128},{16,144},{32,160},{48,176},{64,192},{80,208},{96,224},{112... | collective-permute-start | bytes 393224 | tf_op jit(solution)/shard_map/ppermute | solution.py:269
  12.6 13.2 %collective-permute-start.3 = (bf16[256,256]{1,0:T(8,128)(2,1)S(1)}, bf16[256,256]{1,0:T(8,128)(2,1)S(1)}, u32[]{:S(2)}, u32[]{:S(2)}) collective-permute-start(bf16[256,256]{1,0:T(8,128)(2,1)S(1)} %get-tuple-element.17.refs_0_), channel_id=1, source_target_pairs={{0,32},{16,48},{32,0},{48,16},{64,96},{80,112},{96,64},{112,80},{1... | collective-permute-start | bytes 393224 | tf_op jit(solution)/shard_map/ppermute | solution.py:265
  19.5 20.5 %collective-permute-start = (bf16[256,1024]{1,0:T(8,128)(2,1)}, bf16[256,1024]{1,0:T(8,128)(2,1)S(1)}, u32[]{:S(2)}, u32[]{:S(2)}) collective-permute-start(bf16[256,1024]{1,0:T(8,128)(2,1)} %get-tuple-element.15), channel_id=1, source_target_pairs={{0,64},{16,80},{32,96},{48,112},{64,0},{80,16},{96,32},{112,48},{1... | collective-permute-start | bytes 1572872 | tf_op jit(solution)/shard_map/ppermute | solution.py:269
  21.6 6.3 %collective-permute-start.2 = (bf16[256,256]{1,0:T(8,128)(2,1)S(1)}, bf16[256,256]{1,0:T(8,128)(2,1)S(1)}, u32[]{:S(2)}, u32[]{:S(2)}) collective-permute-start(bf16[256,256]{1,0:T(8,128)(2,1)S(1)} %get-tuple-element.17.refs_0_), channel_id=1, source_target_pairs={{0,48},{16,0},{32,16},{48,32},{64,112},{80,64},{96,80},{112,96},{1... | collective-permute-start | bytes 393224 | tf_op jit(solution)/shard_map/ppermute | solution.py:265
  22.8 9.5 %collective-permute-start.1 = (bf16[256,256]{1,0:T(8,128)(2,1)S(1)}, bf16[256,256]{1,0:T(8,128)(2,1)S(1)}, u32[]{:S(2)}, u32[]{:S(2)}) collective-permute-start(bf16[256,256]{1,0:T(8,128)(2,1)S(1)} %get-tuple-element.17.refs_0_), channel_id=1, source_target_pairs={{0,16},{16,32},{32,48},{48,0},{64,80},{80,96},{96,112},{112,64},{1... | collective-permute-start | bytes 393224 | tf_op jit(solution)/shard_map/ppermute | solution.py:265
  23.8 12.1 %collective-permute-start.7 = (bf16[256,256]{1,0:T(8,128)(2,1)S(1)}, bf16[256,256]{1,0:T(8,128)(2,1)S(1)}, u32[]{:S(2)}, u32[]{:S(2)}) collective-permute-start(bf16[256,256]{1,0:T(8,128)(2,1)S(1)} %collective-permute-done.4.refs_4_), channel_id=1, source_target_pairs={{0,32},{16,48},{32,0},{48,16},{64,96},{80,112},{96,64},{112,80},{1... | collective-permute-start | bytes 393224 | tf_op jit(solution)/shard_map/ppermute | solution.py:265
  25.8 11.1 %collective-permute-start.6 = (bf16[256,256]{1,0:T(8,128)(2,1)S(1)}, bf16[256,256]{1,0:T(8,128)(2,1)S(1)}, u32[]{:S(2)}, u32[]{:S(2)}) collective-permute-start(bf16[256,256]{1,0:T(8,128)(2,1)S(1)} %collective-permute-done.4.refs_4_), channel_id=1, source_target_pairs={{0,48},{16,0},{32,16},{48,32},{64,112},{80,64},{96,80},{112,96},{1... | collective-permute-start | bytes 393224 | tf_op jit(solution)/shard_map/ppermute | solution.py:265
  27.9 12.1 %collective-permute-start.5 = (bf16[256,256]{1,0:T(8,128)(2,1)S(1)}, bf16[256,256]{1,0:T(8,128)(2,1)S(1)}, u32[]{:S(2)}, u32[]{:S(2)}) collective-permute-start(bf16[256,256]{1,0:T(8,128)(2,1)S(1)} %collective-permute-done.4.refs_4_), channel_id=1, source_target_pairs={{0,16},{16,32},{32,48},{48,0},{64,80},{80,96},{96,112},{112,64},{1... | collective-permute-start | bytes 393224 | tf_op jit(solution)/shard_map/ppermute | solution.py:265
  32.3 42.4 %collective-permute-start.15 = (bf16[512,128]{1,0:T(8,128)(2,1)S(1)}, bf16[512,128]{1,0:T(8,128)(2,1)S(1)}, u32[]{:S(2)}, u32[]{:S(2)}) collective-permute-start(bf16[512,128]{1,0:T(8,128)(2,1)S(1)} %reshape_squeeze.3.q_ref), channel_id=1, source_target_pairs={{0,65},{1,64},{16,81},{17,80},{32,97},{33,96},{48,113},{49,112},{6... | collective-permute-start | bytes 393224 | tf_op jit(solution)/shard_map/ppermute | solution.py:278
  35.8 38.9 %collective-permute-start.14 = (bf16[512,128]{1,0:T(8,128)(2,1)S(1)}, bf16[512,128]{1,0:T(8,128)(2,1)S(1)}, u32[]{:S(2)}, u32[]{:S(2)}) collective-permute-start(bf16[512,128]{1,0:T(8,128)(2,1)S(1)} %reshape_squeeze.3.q_ref), channel_id=1, source_target_pairs={{0,1},{1,0},{16,17},{17,16},{32,33},{33,32},{48,49},{49,48},{64,65... | collective-permute-start | bytes 393224 | tf_op jit(solution)/shard_map/ppermute | solution.py:278
  36.9 23.7 %collective-permute-start.12 = (bf16[2,256,256]{2,1,0:T(8,128)(2,1)S(1)}, bf16[2,256,256]{2,1,0:T(8,128)(2,1)S(1)}, u32[]{:S(2)}, u32[]{:S(2)}) collective-permute-start(bf16[2,256,256]{2,1,0:T(8,128)(2,1)S(1)} %pad_maximum_fusion.refs_0_.refs_8_), channel_id=1, source_target_pairs={{0,32},{16,48},{32,0},{48,16},{64,96},{80,112},{96,64},{112,80},{1... | collective-permute-start | bytes 786440 | tf_op jit(solution)/shard_map/ppermute | solution.py:265
  40.0 20.6 %copy-start.5 = (bf16[256,256]{1,0:T(8,128)(2,1)}, bf16[256,256]{1,0:T(8,128)(2,1)S(1)}, u32[]{:S(2)}) copy-start(bf16[256,256]{1,0:T(8,128)(2,1)S(1)} %collective-permute-done.5.refs_5_) | copy-start | bytes 393220
  40.0 20.6 %collective-permute-start.11 = (bf16[2,256,256]{2,1,0:T(8,128)(2,1)S(1)}, bf16[2,256,256]{2,1,0:T(8,128)(2,1)S(1)}, u32[]{:S(2)}, u32[]{:S(2)}) collective-permute-start(bf16[2,256,256]{2,1,0:T(8,128)(2,1)S(1)} %pad_maximum_fusion.refs_0_.refs_8_), channel_id=1, source_target_pairs={{0,48},{16,0},{32,16},{48,32},{64,112},{80,64},{96,80},{112,96},{1... | collective-permute-start | bytes 786440 | tf_op jit(solution)/shard_map/ppermute | solution.py:265
  40.0 20.6 %collective-permute-start.10 = (bf16[2,256,256]{2,1,0:T(8,128)(2,1)S(1)}, bf16[2,256,256]{2,1,0:T(8,128)(2,1)S(1)}, u32[]{:S(2)}, u32[]{:S(2)}) collective-permute-start(bf16[2,256,256]{2,1,0:T(8,128)(2,1)S(1)} %pad_maximum_fusion.refs_0_.refs_8_), channel_id=1, source_target_pairs={{0,16},{16,32},{32,48},{48,0},{64,80},{80,96},{96,112},{112,64},{1... | collective-permute-start | bytes 786440 | tf_op jit(solution)/shard_map/ppermute | solution.py:265
  60.6 14.2 %copy-start.6 = (bf16[256,256]{1,0:T(8,128)(2,1)S(1)}, bf16[256,256]{1,0:T(8,128)(2,1)}, u32[]{:S(2)}) copy-start(bf16[256,256]{1,0:T(8,128)(2,1)} %copy-done.5) | copy-start | bytes 393220
  72.4 27.2 %collective-permute-start.13 = (bf16[256,1024]{1,0:T(8,128)(2,1)S(1)}, bf16[256,1024]{1,0:T(8,128)(2,1)S(1)}, u32[]{:S(2)}, u32[]{:S(2)}) collective-permute-start(bf16[256,1024]{1,0:T(8,128)(2,1)S(1)} %shard_map.106), channel_id=1, source_target_pairs={{0,64},{16,80},{32,96},{48,112},{64,0},{80,16},{96,32},{112,48},{1... | collective-permute-start | bytes 1572872 | tf_op jit(solution)/shard_map/ppermute | solution.py:269
  75.7 35.9 %collective-permute-start.16 = (bf16[528,128]{1,0:T(8,128)(2,1)S(1)}, bf16[528,128]{1,0:T(8,128)(2,1)S(1)}, u32[]{:S(2)}, u32[]{:S(2)}) collective-permute-start(bf16[528,128]{1,0:T(8,128)(2,1)S(1)} %get-tuple-element.12), channel_id=1, source_target_pairs={{0,1},{1,0},{16,17},{17,16},{32,33},{33,32},{48,49},{49,48},{64,65... | collective-permute-start | bytes 405512 | tf_op jit(solution)/shard_map/ppermute | solution.py:278
  84.0 27.6 %collective-permute-start.17 = (bf16[528,128]{1,0:T(8,128)(2,1)S(1)}, bf16[528,128]{1,0:T(8,128)(2,1)S(1)}, u32[]{:S(2)}, u32[]{:S(2)}) collective-permute-start(bf16[528,128]{1,0:T(8,128)(2,1)S(1)} %get-tuple-element.13), channel_id=1, source_target_pairs={{0,65},{1,64},{16,81},{17,80},{32,97},{33,96},{48,113},{49,112},{6... | collective-permute-start | bytes 405512 | tf_op jit(solution)/shard_map/ppermute | solution.py:278
  87.8 13.0 %copy-start.3 = (f32[8192]{0:T(1024)S(1)}, f32[8192]{0:T(1024)}, u32[]{:S(2)}) copy-start(f32[8192]{0:T(1024)} %param.14) | copy-start | bytes 98308
  99.6 2.0 %copy-start.1 = (bf16[1,1,16,256,256]{4,3,2,1,0:T(8,128)(2,1)S(1)}, bf16[1,1,16,256,256]{4,3,2,1,0:T(8,128)(2,1)}, u32[]{:S(2)}) copy-start(bf16[1,1,16,256,256]{4,3,2,1,0:T(8,128)(2,1)} %param.12) | copy-start | bytes 6291460
  101.6 2.2 %copy-start = (bf16[8192,256]{1,0:T(8,128)(2,1)S(1)}, bf16[8192,256]{1,0:T(8,128)(2,1)}, u32[]{:S(2)}) copy-start(bf16[8192,256]{1,0:T(8,128)(2,1)} %weight_ref.1) | copy-start | bytes 12582916
  103.8 1.2 %copy-start.2 = (bf16[8,64,1024]{2,1,0:T(8,128)(2,1)S(1)}, bf16[8,64,1024]{2,1,0:T(8,128)(2,1)}, u32[]{:S(2)}) copy-start(bf16[8,64,1024]{2,1,0:T(8,128)(2,1)} %all-gather.2.cloned.1.call-done.hidden_ref) | copy-start | bytes 3145732
Sparse Core Ops, SparseCore 0:
  17.6 24.4 all-gather.1

commit v2 on v1

--- a/solution.py
+++ b/solution.py
@@ -11,10 +11,11 @@
 HD = 128
 GROUP = 8
 BLOCK = 256
+DECODE_ROWS = 64
 MASKED = -1e30
 LOG2E = 1.4426950408889634
 SCALE2 = HD ** (-0.5) * LOG2E
-VMEM_LIMIT = 40 * 1024 * 1024
+MIB = 1024 * 1024
 
 bf16 = jnp.bfloat16
 f32 = jnp.float32
@@ -93,7 +94,7 @@
             stat_ref[side] = jnp.where(lane == h + 8, mixed[:, HD:], old)
             return carry
 
-        lax.fori_loop(0, GROUP, head, 0)
+        lax.fori_loop(0, GROUP, head, 0, unroll=4)
 
 
 def last_kernel(info, q_ref, acc_ref, stat_ref, *refs):
@@ -121,7 +122,7 @@
             out_ref[:, at] = ((acc_ref[0, h] * fade + mixed[:, :HD]) / total).astype(bf16)
             return carry
 
-        lax.fori_loop(0, GROUP, head, 0)
+        lax.fori_loop(0, GROUP, head, 0, unroll=4)
 
     @pl.when(info[2] < 2)
     def _():
@@ -133,103 +134,131 @@
         lax.fori_loop(0, GROUP, head, 0)
 
 
-def segment_kernel(info, q0_ref, q1_ref, *refs):
+def segment_kernel(info, rows_ref, *refs):
     near = refs[:8]
     far = refs[8:12]
-    out0_ref, out1_ref, aug_scr = refs[12:]
-
-    def keys(b):
+    out_ref, aug_scr = refs[12:]
+
+    def block_of(b, at):
         if b < 8:
-            return near[b][:, :HD]
-        return far[(b - 8) // 2][(b - 8) % 2, :, :HD]
+            return near[b][:, at]
+        return far[(b - 8) // 2][(b - 8) % 2, :, at]
 
     for b in range(16):
-        block = near[b][...] if b < 8 else far[(b - 8) // 2][(b - 8) % 2]
-        fill_values(aug_scr, b, block)
-    for which, (q_ref, out_ref) in enumerate(((q0_ref, out0_ref), (q1_ref, out1_ref))):
+        aug_scr[b, :, :HD] = block_of(b, slice(HD, 2 * HD))
+        aug_scr[b, :, HD:] = jnp.ones((BLOCK, HD), bf16)
+    lane = lax.broadcasted_iota(jnp.int32, (DECODE_ROWS, HD), 1)
+
+    for which in range(2):
 
         @pl.when(info[3 + which] == 1)
         def _():
-            pieces = []
+            stat = jnp.zeros((DECODE_ROWS, HD), f32)
             for tile in range(2):
-                rows = q_ref[tile * 256 : tile * 256 + 256]
-                parts = [scores_of(rows, keys(b)) for b in range(16)]
-                highest = max_of(parts)
-                mixed = weigh(parts, highest, [aug_scr[b] for b in range(16)])
+                heads = range(tile * 4, tile * 4 + 4)
+                rows = jnp.concatenate(
+                    [rows_ref[which, :, h * HD : (h + 1) * HD] for h in heads], axis=0
+                )
+                highest = None
+                for chunk in range(4):
+                    blocks = range(chunk * 4, chunk * 4 + 4)
+                    parts = [scores_of(rows, block_of(b, slice(0, HD))) for b in blocks]
+                    top = max_of(parts)
+                    if highest is None:
+                        mixed = weigh(parts, top, [aug_scr[b] for b in blocks])
+                    else:
+                        top = jnp.maximum(top, highest)
+                        mixed = mixed * jnp.exp2((highest - top) * SCALE2) + weigh(
+                            parts, top, [aug_scr[b] for b in blocks]
+                        )
+                    highest = top
                 total = mixed[:, HD:]
-                out_ref[tile * 256 : tile * 256 + 256] = (mixed[:, :HD] / total).astype(bf16)
+                share = (mixed[:, :HD] / total).astype(bf16)
                 level = highest * SCALE2 + jnp.log2(total)
-                turned = jnp.transpose(level)[0:1]
-                pieces += [turned[:, :128], turned[:, 128:]]
-            level = jnp.concatenate(pieces, axis=0)
-            high = level.astype(bf16)
-            rest = level - high.astype(f32)
-            middle = rest.astype(bf16)
-            low = (rest - middle.astype(f32)).astype(bf16)
-            out_ref[512:528] = jnp.concatenate(
-                [high.astype(f32), middle.astype(f32), low.astype(f32), jnp.zeros((4, HD), f32)],
-                axis=0,
-            ).astype(bf16)
+                for i, h in enumerate(heads):
+                    at = slice(i * DECODE_ROWS, (i + 1) * DECODE_ROWS)
+                    out_ref[which, :, h * HD : (h + 1) * HD] = share[at]
+                    stat = jnp.where(lane == h, level[at], stat)
+            high = stat.astype(bf16).astype(f32)
+            middle = (stat - high).astype(bf16).astype(f32)
+            low = stat - high - middle
+            pieces = high + pltpu.roll(middle, 8, 1) + pltpu.roll(low, 16, 1)
+            out_ref[which, :, GROUP * HD :] = pieces.astype(bf16)
 
         @pl.when(info[3 + which] != 1)
         def _():
-            out_ref[...] = jnp.zeros_like(out_ref)
+            out_ref[which] = jnp.zeros((DECODE_ROWS, (GROUP + 1) * HD), bf16)
 
 
 def local_kernel(
-    len_ref, hidden_ref, gain_ref, weight_ref, cos_ref, sin_ref, q_ref, cache_ref, out_ref, level_ref
+    info, len_ref, cos_ref, sin_ref, gain_ref, q_ref, near_ref, far_ref, weight_ref, cache_ref,
+    out_ref, level_ref,
 ):
-    width = hidden_ref.shape[2]
-    squares = jnp.zeros((64, 1), f32)
-    projected = jnp.zeros((64, 2 * HD), f32)
-    for part in range(D // width):
-        wide = hidden_ref[part].astype(f32)
-        squares = squares + jnp.sum(wide * wide, axis=-1, keepdims=True)
-        scaled = (wide * gain_ref[:, part * width : (part + 1) * width]).astype(bf16)
-        projected = projected + jnp.dot(
-            scaled, weight_ref[part * width : (part + 1) * width], preferred_element_type=f32
-        )
+    width = near_ref.shape[2]
+    core, x = info[6], info[7]
+    squares = jnp.zeros((DECODE_ROWS, 1), f32)
+    projected = jnp.zeros((DECODE_ROWS, 2 * HD), f32)
+    for side, part_ref in enumerate((near_ref, far_ref)):
+        for i, step in enumerate((0, 3, 1, 2)):
+            owner = ((x + step) % 4) * 2 + (core if side == 0 else 1 - core)
+            wide = part_ref[i].astype(f32)
+            squares = squares + jnp.sum(wide * wide, axis=-1, keepdims=True)
+            scaled = (wide * gain_ref[pl.ds(owner, 1)]).astype(bf16)
+            projected = projected + jnp.dot(
+                scaled,
+                weight_ref[pl.ds(pl.multiple_of(owner * width, width), width)],
+                preferred_element_type=f32,
+            )
     normed = projected * lax.rsqrt(squares / D + 1e-6)
     key_rows = normed[:, :HD]
-    turned = jnp.concatenate([key_rows[:, HD // 2 :], key_rows[:, : HD // 2]], axis=1)
+    turned = pltpu.roll(key_rows, HD // 2, 1)
     fresh_k = (key_rows * cos_ref[...] + turned * sin_ref[...]).astype(bf16)
     fresh_v = normed[:, HD:].astype(bf16)
-    fresh_aug = jnp.concatenate([fresh_v, jnp.ones((64, HD), bf16)], axis=1)
+    fresh_aug = jnp.concatenate([fresh_v, jnp.ones((DECODE_ROWS, HD), bf16)], axis=1)
     ones = jnp.ones((BLOCK, HD), bf16)
-    slot = lax.broadcasted_iota(jnp.int32, (32, BLOCK), 1)
-    fresh_slot = lax.broadcasted_iota(jnp.int32, (32, 64), 1)
-    step = lax.broadcasted_iota(jnp.int32, (32, 64), 0) // GROUP
-
-    for s in range(16):
-        rows = q_ref[s * 32 : (s + 1) * 32]
-        cache_part = jnp.where(
-            slot < len_ref[s], scores_of(rows, cache_ref[s, :, :HD]), MASKED
-        )
-        allowed = (fresh_slot >= s * 4) & (fresh_slot <= s * 4 + step)
+    row = lax.broadcasted_iota(jnp.int32, (128, BLOCK), 0)
+    slot = lax.broadcasted_iota(jnp.int32, (128, BLOCK), 1)
+    fresh_row = lax.broadcasted_iota(jnp.int32, (128, DECODE_ROWS), 0) % 16
+    fresh_slot = lax.broadcasted_iota(jnp.int32, (128, DECODE_ROWS), 1)
+
+    for g in range(4):
+        at = slice(g * 16, (g + 1) * 16)
+        rows = jnp.concatenate([q_ref[at, h * HD : (h + 1) * HD] for h in range(GROUP)], axis=0)
+        parts = []
+        augs = []
+        for j in range(4):
+            s = g * 4 + j
+            allowed = (row % 16 // 4 == j) & (slot < len_ref[s])
+            parts.append(jnp.where(allowed, scores_of(rows, cache_ref[s, :, :HD]), MASKED))
+            augs.append(jnp.concatenate([cache_ref[s, :, HD:], ones], axis=1))
+        behind = fresh_row + g * 16 - fresh_slot
+        allowed = (behind >= 0) & (behind <= fresh_row % 4)
         fresh_part = jnp.where(allowed, scores_of(rows, fresh_k), MASKED)
-        highest = jnp.maximum(
-            jnp.max(cache_part, axis=-1, keepdims=True), jnp.max(fresh_part, axis=-1, keepdims=True)
-        )
-        cache_aug = jnp.concatenate([cache_ref[s, :, HD:], ones], axis=1)
-        mixed = weigh([cache_part, fresh_part], highest, [cache_aug, fresh_aug])
+        highest = jnp.maximum(max_of(parts), jnp.max(fresh_part, axis=-1, keepdims=True))
+        mixed = weigh(parts + [fresh_part], highest, augs + [fresh_aug])
         total = mixed[:, HD:]
-        out_ref[s * 32 : (s + 1) * 32] = mixed[:, :HD] / total
-        level_ref[s * 32 : (s + 1) * 32] = highest * SCALE2 + jnp.log2(total)
+        share = mixed[:, :HD] / total
+        level = highest * SCALE2 + jnp.log2(total)
+        for h in range(GROUP):
+            out_ref[at, h * HD : (h + 1) * HD] = share[h * 16 : (h + 1) * 16]
+            level_ref[at, h * HD : (h + 1) * HD] = level[h * 16 : (h + 1) * 16]
 
 
 def merge_kernel(info, local_ref, level_ref, same_ref, other_ref, out_ref):
+    lane = lax.broadcasted_iota(jnp.int32, (DECODE_ROWS, HD), 1)
+
     def merge(part_ref):
-        stat = part_ref[512:528].astype(f32)
-        level = stat[0:4] + stat[4:8] + stat[8:12]
-        for tile in range(4):
-            at = slice(tile * 128, tile * 128 + 128)
-            far = jnp.transpose(jnp.broadcast_to(level[tile : tile + 1], (128, 128)))
-            near = level_ref[at]
+        pieces = part_ref[:, GROUP * HD :].astype(f32)
+        for h in range(GROUP):
+            at = slice(h * HD, (h + 1) * HD)
+            mine = (lane == h) | (lane == h + 8) | (lane == h + 16)
+            far = jnp.sum(jnp.where(mine, pieces, 0.0), axis=-1, keepdims=True)
+            near = level_ref[:, at]
             top = jnp.maximum(far, near)
             far_share = jnp.exp2(far - top)
             near_share = jnp.exp2(near - top)
-            mixed = part_ref[at].astype(f32) * far_share + local_ref[at] * near_share
-            out_ref[at] = (mixed / (far_share + near_share)).astype(bf16)
+            mixed = part_ref[:, at].astype(f32) * far_share + local_ref[:, at] * near_share
+            out_ref[:, at] = (mixed / (far_share + near_share)).astype(bf16)
 
     @pl.when(info[5] == 1)
     def _():
@@ -244,7 +273,7 @@
 VMEM = pl.BlockSpec(memory_space=pltpu.VMEM)
 
 
-def call(kernel, out_shape, args, scalars=1, scratch=(), flops=0, touched=0, exps=0, specs=None):
+def call(kernel, out_shape, args, scalars=1, scratch=(), flops=0, touched=0, exps=0, specs=None, vmem=24):
     in_specs = [SMEM] * scalars + [VMEM] * (len(args) - scalars)
     for place, spec in (specs or {}).items():
         in_specs[place] = spec
@@ -255,7 +284,7 @@
         in_specs=in_specs,
         out_specs=jax.tree.map(lambda _: VMEM, out_shape),
         scratch_shapes=list(scratch),
-        compiler_params=pltpu.CompilerParams(vmem_limit_bytes=VMEM_LIMIT),
+        compiler_params=pltpu.CompilerParams(vmem_limit_bytes=vmem * MIB),
         cost_estimate=pl.CostEstimate(flops=flops, bytes_accessed=touched, transcendentals=exps),
     )(*args)
 
@@ -271,6 +300,10 @@
 
 def y_all(block):
     return [block, y_turn(block, 1), y_turn(block, -1), y_turn(block, 2)]
+
+
+def tp_turn(block, distance):
+    return lax.ppermute(block, "tp", [(i, (i + distance) % 8) for i in range(8)])
 
 
 def pool_swap(block, z_bits):
@@ -305,6 +338,8 @@
             (here[place] == parity).astype(jnp.int32),
             (here[place ^ 4] == parity).astype(jnp.int32),
             (there[place] == parity).astype(jnp.int32),
+            lax.axis_index("tp") % 2,
+            lax.axis_index("tp") // 2,
         ]
     ).astype(jnp.int32)
 
@@ -323,10 +358,12 @@
 
     hidden = new_hidden[0, 0]
     samples, steps, width = hidden.shape
-    wide = lax.all_gather(hidden.reshape(samples * steps, width), "tp", axis=0)
-    step_rows = decode_query[0, 0].reshape(samples * steps * GROUP, HD)
-    rows0 = pool_swap(step_rows, 0)
-    rows1 = pool_swap(step_rows, 1)
+    decode_rows = samples * steps
+    hidden = hidden.reshape(decode_rows, width)
+    near = jnp.stack([hidden, tp_turn(hidden, 2), tp_turn(hidden, -2), tp_turn(hidden, 4)])
+    far = lax.ppermute(near, "tp", [(i, i ^ 1) for i in range(8)])
+    step_rows = decode_query[0, 0].reshape(decode_rows, width)
+    rows_pair = pool_swap(jnp.stack([step_rows, z_swap(step_rows, 1)]), 0)
 
     lengths = cached_len[0, 0]
     half = HD // 2
@@ -338,23 +375,25 @@
     sin_all = jnp.concatenate([-sine, sine], axis=-1)
 
     shape = jax.ShapeDtypeStruct
-    rows = samples * steps * GROUP
     local_out, local_level = call(
         local_kernel,
-        (shape((rows, HD), f32), shape((rows, HD), f32)),
+        (shape((decode_rows, width), f32), shape((decode_rows, width), f32)),
         (
+            info,
             lengths,
-            wide,
-            norm_gain[None],
-            kv_weight,
             cos_all,
             sin_all,
+            norm_gain.reshape(D // width, width),
             step_rows,
+            near,
+            far,
+            kv_weight,
             gen_cache[0, 0],
         ),
+        scalars=2,
         flops=2 * 64 * D * 256,
         touched=8 << 20,
-        exps=rows * 320,
+        exps=512 * 320,
     )
 
     acc, stat = call(
@@ -370,17 +409,17 @@
         touched=4 << 20,
         exps=3 * 2048 * 1024,
     )
-    segment0, segment1 = call(
+    segment_pair = call(
         segment_kernel,
-        (shape((rows + 16, HD), bf16), shape((rows + 16, HD), bf16)),
-        (info, rows0, rows1, *group0, *group1, *group23),
+        shape((2, decode_rows, width + HD), bf16),
+        (info, rows_pair, *group0, *group1, *group23),
         scratch=(pltpu.VMEM((16, BLOCK, 2 * HD), bf16),),
         flops=1024 * 4096 * 512,
         touched=3 << 20,
         exps=1024 * 4096,
     )
-    back0 = pool_swap(segment0, 0)
-    back1 = pool_swap(segment1, 1)
+    back0 = pool_swap(segment_pair[0], 0)
+    back1 = pool_swap(segment_pair[1], 1)
 
     def finish(q_rows, side):
         return call(
@@ -402,13 +441,13 @@
     out_own = finish(q_keep, 0)
     merged = call(
         merge_kernel,
-        shape((rows, HD), bf16),
+        shape((decode_rows, width), bf16),
         (info, local_out, local_level, back0, back1),
-        flops=rows * HD * 8,
+        flops=512 * HD * 8,
         touched=1 << 20,
-        exps=rows * HD * 2,
-    )
-    decode_out = merged.reshape(samples, steps, GROUP * HD)
+        exps=512 * HD * 2,
+    )
+    decode_out = merged.reshape(samples, steps, width)
     segment_out = jnp.where(
         even, jnp.stack([out_own, returned]), jnp.stack([returned, out_own])
     )

time: 120 us -> 103 us (0.86)
  the two profiles are of different devices: /device:TPU:70 before, /device:TPU:80 now
where the time goes in v2:
time: 103 us; the launch traced here: 102 us
  Pallas kernels  38 us (37%)
  starting transfers between devices  34.6 us (34%)
  waiting for transfers between devices  12.7 us (12%)
  local copies, waits for them, and re-layouts  7.45 us (7%)
  other arithmetic  6.47 us (6%)
  between operations  2.84 us (3%)
    pallas_call x6, Pallas kernels, call(): pl.pallas_call(kernel, grid=(1,) if specs else (), out_shape=out_shape, i...  38 us
    ppermute x3, starting transfers between devices, pool_swap(): return lax.ppermute(block, ('ctx', 'pd'), route)  11.4 us
    ppermute x9, starting transfers between devices, y_turn(): return lax.ppermute(block, 'ctx', route)  11.2 us
    ppermute x3, waiting for transfers between devices, pool_swap(): return lax.ppermute(block, ('ctx', 'pd'), route)  10.7 us
    ppermute x6, starting transfers between devices, z_swap(): return lax.ppermute(block, 'ctx', [(i, i ^ 4 * bits) for i in range(16)])  6.7 us
    ppermute x3, starting transfers between devices, tp_turn(): lax.ppermute(block, 'tp', [(i, (i + distance) % 8) for i in range(8)])  5.14 us
    select_n x1, other arithmetic, on_device(): q_keep = jnp.where(even, queries[0], queries[1])  2.07 us
  transfers between devices with their start and end apart: 22, of which 4 were waited for; matrix products, arithmetic and copies ran while one was open for 10% of the time, Pallas kernels for 37%

profile of v2, /device:TPU:80, one launch (start us, length us, event | category | flops | bytes accessed | tf_op | source)
XLA Modules:
  0.0 102.1 jit_solution(12710592710977760458)
XLA Ops:
  0.7 1.0 reshape_squeeze.7
  1.6 3.1 %collective-permute-start.16 = (bf16[64,1024]{1,0:T(8,128)(2,1)S(1)}, bf16[64,1024]{1,0:T(8,128)(2,1)}, u32[]{:S(2)}, u32[]{:S(2)}) collective-permute-start(bf16[64,1024]{1,0:T(8,128)(2,1)S(1)} %reshape_squeeze.7), channel_id=1, source_target_pairs={{0,8},{2,10},{4,12},{6,14},{8,0},{10,2},{12,4},{14,6},{1,9},{3,11}... | collective-permute-start | bytes 393224 | tf_op jit(solution)/shard_map/ppermute | solution.py:306
  4.7 1.1 %collective-permute-start.15 = (bf16[64,1024]{1,0:T(8,128)(2,1)S(1)}, bf16[64,1024]{1,0:T(8,128)(2,1)}, u32[]{:S(2)}, u32[]{:S(2)}) collective-permute-start(bf16[64,1024]{1,0:T(8,128)(2,1)S(1)} %reshape_squeeze.7), channel_id=1, source_target_pairs={{0,12},{2,14},{4,0},{6,2},{8,4},{10,6},{12,8},{14,10},{1,13},{3,15... | collective-permute-start | bytes 393224 | tf_op jit(solution)/shard_map/ppermute | solution.py:306
  5.9 0.9 collective-permute-start.14
  6.8 0.9 reshape_squeeze.6.q_ref
  7.7 2.0 %collective-permute-start.18 = (bf16[64,1024]{1,0:T(8,128)(2,1)S(1)}, bf16[64,1024]{1,0:T(8,128)(2,1)S(1)}, u32[]{:S(2)}, u32[]{:S(2)}) collective-permute-start(bf16[64,1024]{1,0:T(8,128)(2,1)S(1)} %reshape_squeeze.6.q_ref), channel_id=1, source_target_pairs={{0,64},{16,80},{32,96},{48,112},{64,0},{80,16},{96,32},{112,48},{1... | collective-permute-start | bytes 393224 | tf_op jit(solution)/shard_map/ppermute | solution.py:298
  9.7 1.0 select_bitcast_fusion.2
  10.8 2.1 %select_bitcast_fusion.1 = (bf16[256,1024]{1,0:T(8,128)(2,1)S(1)}, bf16[256,1024]{1,0:T(8,128)(2,1)}) fusion(pred[]{:T(512)S(6)} %eq.16, bf16[1,2,256,1024]{3,2,1,0:T(8,128)(2,1)} %param.9), kind=kLoop, calls=%fused_computation.3 | loop fusion | flops 524288 | bytes 2097153 | tf_op jit(solution)/shard_map/jit(_where)/select_n | solution.py:353
  12.9 1.1 %collective-permute-done.18 = bf16[64,1024]{1,0:T(8,128)(2,1)S(1)} collective-permute-done((bf16[64,1024]{1,0:T(8,128)(2,1)S(1)}, bf16[64,1024]{1,0:T(8,128)(2,1)S(1)}, u32[]{:S(2)}, u32[]{:S(2)}) %collective-permute-start.18) | collective-permute-done | bytes 131104 | tf_op jit(solution)/shard_map/ppermute | solution.py:298
  14.0 2.3 %collective-permute-start.4 = (bf16[256,256]{1,0:T(8,128)(2,1)S(1)}, bf16[256,256]{1,0:T(8,128)(2,1)S(1)}, u32[]{:S(2)}, u32[]{:S(2)}) collective-permute-start(bf16[256,256]{1,0:T(8,128)(2,1)S(1)} %get-tuple-element.14), channel_id=1, source_target_pairs={{0,64},{16,80},{32,96},{48,112},{64,0},{80,16},{96,32},{112,48},{1... | collective-permute-start | bytes 393224 | tf_op jit(solution)/shard_map/ppermute | solution.py:298
  17.0 2.5 %collective-permute-start.2 = (bf16[256,256]{1,0:T(8,128)(2,1)S(1)}, bf16[256,256]{1,0:T(8,128)(2,1)S(1)}, u32[]{:S(2)}, u32[]{:S(2)}) collective-permute-start(bf16[256,256]{1,0:T(8,128)(2,1)S(1)} %get-tuple-element.15.refs_0_), channel_id=1, source_target_pairs={{0,48},{16,0},{32,16},{48,32},{64,112},{80,64},{96,80},{112,96},{1... | collective-permute-start | bytes 393224 | tf_op jit(solution)/shard_map/ppermute | solution.py:294
  20.1 1.3 %collective-permute-start.1 = (bf16[256,256]{1,0:T(8,128)(2,1)S(1)}, bf16[256,256]{1,0:T(8,128)(2,1)S(1)}, u32[]{:S(2)}, u32[]{:S(2)}) collective-permute-start(bf16[256,256]{1,0:T(8,128)(2,1)S(1)} %get-tuple-element.15.refs_0_), channel_id=1, source_target_pairs={{0,16},{16,32},{32,48},{48,0},{64,80},{80,96},{96,112},{112,64},{1... | collective-permute-start | bytes 393224 | tf_op jit(solution)/shard_map/ppermute | solution.py:294
  21.3 1.0 collective-permute-start.7
  22.4 1.6 %collective-permute-start.6 = (bf16[256,256]{1,0:T(8,128)(2,1)S(1)}, bf16[256,256]{1,0:T(8,128)(2,1)S(1)}, u32[]{:S(2)}, u32[]{:S(2)}) collective-permute-start(bf16[256,256]{1,0:T(8,128)(2,1)S(1)} %collective-permute-done.4.refs_4_), channel_id=1, source_target_pairs={{0,48},{16,0},{32,16},{48,32},{64,112},{80,64},{96,80},{112,96},{1... | collective-permute-start | bytes 393224 | tf_op jit(solution)/shard_map/ppermute | solution.py:294
  25.6 2.1 %collective-permute-start = (bf16[256,1024]{1,0:T(8,128)(2,1)}, bf16[256,1024]{1,0:T(8,128)(2,1)S(1)}, u32[]{:S(2)}, u32[]{:S(2)}) collective-permute-start(bf16[256,1024]{1,0:T(8,128)(2,1)} %get-tuple-element.11), channel_id=1, source_target_pairs={{0,64},{16,80},{32,96},{48,112},{64,0},{80,16},{96,32},{112,48},{1... | collective-permute-start | bytes 1572872 | tf_op jit(solution)/shard_map/ppermute | solution.py:298
  27.7 1.3 %collective-permute-start.12 = (bf16[2,256,256]{2,1,0:T(8,128)(2,1)S(1)}, bf16[2,256,256]{2,1,0:T(8,128)(2,1)S(1)}, u32[]{:S(2)}, u32[]{:S(2)}) collective-permute-start(bf16[2,256,256]{2,1,0:T(8,128)(2,1)S(1)} %pad_maximum_fusion.1.refs_0_.refs_8_), channel_id=1, source_target_pairs={{0,32},{16,48},{32,0},{48,16},{64,96},{80,112},{96,64},{112,80},{1... | collective-permute-start | bytes 786440 | tf_op jit(solution)/shard_map/ppermute | solution.py:294
  29.0 2.6 %collective-permute-start.11 = (bf16[2,256,256]{2,1,0:T(8,128)(2,1)S(1)}, bf16[2,256,256]{2,1,0:T(8,128)(2,1)S(1)}, u32[]{:S(2)}, u32[]{:S(2)}) collective-permute-start(bf16[2,256,256]{2,1,0:T(8,128)(2,1)S(1)} %pad_maximum_fusion.1.refs_0_.refs_8_), channel_id=1, source_target_pairs={{0,48},{16,0},{32,16},{48,32},{64,112},{80,64},{96,80},{112,96},{1... | collective-permute-start | bytes 786440 | tf_op jit(solution)/shard_map/ppermute | solution.py:294
  32.3 4.9 %collective-permute-start.19 = (bf16[2,64,1024]{2,1,0:T(8,128)(2,1)}, bf16[2,64,1024]{2,1,0:T(8,128)(2,1)S(1)}, u32[]{:S(2)}, u32[]{:S(2)}) collective-permute-start(bf16[2,64,1024]{2,1,0:T(8,128)(2,1)} %pad_maximum_fusion.2), channel_id=1, source_target_pairs={{0,1},{1,0},{16,17},{17,16},{32,33},{33,32},{48,49},{49,48},{64,65... | collective-permute-start | bytes 786440 | tf_op jit(solution)/shard_map/ppermute | solution.py:311
  37.4 1.6 %stack_reshape_squeeze.6 = bf16[1,64,1024]{2,1,0:T(8,128)(2,1)} reshape(bf16[1,1,16,4,1024]{4,3,2,1,0:T(4,128)(2,1)} %param.13) | data formatting | bytes 262144 | tf_op jit(solution)/shard_map/stack;reshape;squeeze | solution.py:363
  41.6 0.8 reshape.117.gain_ref
  42.5 1.2 %pad_maximum_fusion.near_ref = bf16[4,64,1024]{2,1,0:T(8,128)(2,1)S(1)} fusion(bf16[1,64,1024]{2,1,0:T(8,128)(2,1)} %bitcast.22, bf16[1,64,1024]{2,1,0:T(8,128)(2,1)} %bitcast.21, bf16[1,64,1024]{2,1,0:T(8,128)(2,1)} %bitcast.41, bf16[1,64,1024]{2,1,0:T(8,128)(2,1)} %stack_reshape_squeeze.6), kind=kLoop, calls=%fused_computation.1 | loop fusion | flops 786432 | bytes 1048576 | tf_op jit(solution)/shard_map/stack | solution.py:363
  43.8 10.7 %collective-permute-done.19.rows_ref = bf16[2,64,1024]{2,1,0:T(8,128)(2,1)S(1)} collective-permute-done((bf16[2,64,1024]{2,1,0:T(8,128)(2,1)}, bf16[2,64,1024]{2,1,0:T(8,128)(2,1)S(1)}, u32[]{:S(2)}, u32[]{:S(2)}) %collective-permute-start.19) | collective-permute-done | bytes 262176 | tf_op jit(solution)/shard_map/ppermute | solution.py:311
  54.5 0.9 copy-done.4
  55.4 7.3 %shard_map.108 = bf16[2,64,1152]{2,1,0:T(8,128)(2,1)S(1)} custom-call(s32[8]{0:T(128)S(1)} %stack.88.info, bf16[2,64,1024]{2,1,0:T(8,128)(2,1)S(1)} %collective-permute-done.19.rows_ref, bf16[256,256]{1,0:T(8,128)(2,1)S(1)} %get-tuple-element.15.refs_0_, bf16[256,256]{1,0:T(8,128)(2,1)S(1)} %collective-permute-done.1.refs_1_, ...), custom_call_target="tpu_custom_call" | custom-call | flops 2147483648 | bytes 3145728 | tf_op jit(solution)/shard_map/pallas_call | solution.py:280
  62.8 10.7 %shard_map.104 = (f32[2,8,256,128]{3,2,1,0:T(8,128)S(1)}, f32[2,256,128]{2,1,0:T(8,128)S(1)}) custom-call(s32[8]{0:T(128)S(1)} %stack.88.info, bf16[256,1024]{1,0:T(8,128)(2,1)S(1)} %get-tuple-element.10.own_q.q_ref, bf16[256,1024]{1,0:T(8,128)(2,1)S(1)} %collective-permute-done.partner_q.q_ref, bf16[256,256]{1,0:T(8,128)(2,1)S(1)} %get-tuple-element.15.refs_0_, ...), custom_call_target="tpu_custom_call" | custom-call | flops 3221225472 | bytes 4194304 | tf_op jit(solution)/shard_map/pallas_call | solution.py:280
  73.5 7.4 %shard_map.106 = bf16[256,1024]{1,0:T(8,128)(2,1)S(1)} custom-call(s32[8]{0:T(128)S(1)} %stack.88.info, bf16[256,1024]{1,0:T(8,128)(2,1)S(1)} %collective-permute-done.partner_q.q_ref, f32[2,8,256,128]{3,2,1,0:T(8,128)S(1)} %get-tuple-element.6.acc_ref, f32[2,256,128]{2,1,0:T(8,128)S(1)} %get-tuple-element.7.stat_ref, ...), custom_call_target="tpu_custom_call" | custom-call | flops 2147483648 | bytes 4194304 | tf_op jit(solution)/shard_map/pallas_call | solution.py:280
  81.1 1.2 %collective-permute-start.21 = (bf16[64,1152]{1,0:T(8,128)(2,1)S(1)}, bf16[64,1152]{1,0:T(8,128)(2,1)S(1)}, u32[]{:S(2)}, u32[]{:S(2)}) collective-permute-start(bf16[64,1152]{1,0:T(8,128)(2,1)S(1)} %get-tuple-element.12), channel_id=1, source_target_pairs={{0,65},{1,64},{16,81},{17,80},{32,97},{33,96},{48,113},{49,112},{6... | collective-permute-start | bytes 442376 | tf_op jit(solution)/shard_map/ppermute | solution.py:311
  82.3 5.4 %collective-permute-start.20 = (bf16[64,1152]{1,0:T(8,128)(2,1)S(1)}, bf16[64,1152]{1,0:T(8,128)(2,1)S(1)}, u32[]{:S(2)}, u32[]{:S(2)}) collective-permute-start(bf16[64,1152]{1,0:T(8,128)(2,1)S(1)} %get-tuple-element.13), channel_id=1, source_target_pairs={{0,1},{1,0},{16,17},{17,16},{32,33},{33,32},{48,49},{49,48},{64,65... | collective-permute-start | bytes 442376 | tf_op jit(solution)/shard_map/ppermute | solution.py:311
  87.7 7.7 %shard_map.105 = bf16[256,1024]{1,0:T(8,128)(2,1)S(1)} custom-call(s32[8]{0:T(128)S(1)} %stack.88.info, bf16[256,1024]{1,0:T(8,128)(2,1)S(1)} %get-tuple-element.10.own_q.q_ref, f32[2,8,256,128]{3,2,1,0:T(8,128)S(1)} %get-tuple-element.6.acc_ref, f32[2,256,128]{2,1,0:T(8,128)S(1)} %get-tuple-element.7.stat_ref, ...), custom_call_target="tpu_custom_call" | custom-call | flops 2147483648 | bytes 4194304 | tf_op jit(solution)/shard_map/pallas_call | solution.py:280
  95.4 4.0 %shard_map.107 = (f32[64,1024]{1,0:T(8,128)S(1)}, f32[64,1024]{1,0:T(8,128)S(1)}) custom-call(s32[8]{0:T(128)S(1)} %stack.88.info, s32[16]{0:T(128)S(1)} %bitcast.36, f32[64,128]{1,0:T(8,128)S(1)} %get-tuple-element.22.cos_ref, f32[64,128]{1,0:T(8,128)S(1)} %get-tuple-element.23.sin_ref, f32[8,1024]{1,0:T(8,128)S(1)} %reshape.117.gain_ref, ...), custom_call_target="tpu_custom_call" | custom-call | flops 268435456 | bytes 8388608 | tf_op jit(solution)/shard_map/pallas_call | solution.py:280
  99.5 0.8 shard_map.109
  101.0 1.1 %maximum_select_fusion = bf16[1,2,256,1024]{3,2,1,0:T(8,128)(2,1)} fusion(bf16[1,1,256,1024]{3,2,1,0:T(8,128)(2,1)S(1)} %bitcast.37, bf16[1,1,256,1024]{3,2,1,0:T(8,128)(2,1)S(1)} %bitcast.35, pred[]{:T(512)S(6)} %eq.16), kind=kLoop, calls=%fused_computation | loop fusion | flops 1572864 | bytes 2097153 | tf_op jit(solution)/shard_map/jit(_where)/select_n | solution.py:451
  (55 shorter events, 5.6 us)
Async XLA Ops:
  0.6 16.2 %copy-start.5 = (bf16[1,1,16,4,1024]{4,3,2,1,0:T(4,128)(2,1)S(1)}, bf16[1,1,16,4,1024]{4,3,2,1,0:T(4,128)(2,1)}, u32[]{:S(2)}) copy-start(bf16[1,1,16,4,1024]{4,3,2,1,0:T(4,128)(2,1)} %param.11) | copy-start | bytes 393220
  0.6 12.2 %copy-start.2 = (s32[1,1,16]{2,1,0:T(1,128)S(1)}, s32[1,1,16]{2,1,0:T(1,128)}, u32[]{:S(2)}) copy-start(s32[1,1,16]{2,1,0:T(1,128)} %param.17) | copy-start | bytes 196
  1.6 14.7 %collective-permute-start.16 = (bf16[64,1024]{1,0:T(8,128)(2,1)S(1)}, bf16[64,1024]{1,0:T(8,128)(2,1)}, u32[]{:S(2)}, u32[]{:S(2)}) collective-permute-start(bf16[64,1024]{1,0:T(8,128)(2,1)S(1)} %reshape_squeeze.7), channel_id=1, source_target_pairs={{0,8},{2,10},{4,12},{6,14},{8,0},{10,2},{12,4},{14,6},{1,9},{3,11}... | collective-permute-start | bytes 393224 | tf_op jit(solution)/shard_map/ppermute | solution.py:306
  4.7 11.7 %collective-permute-start.15 = (bf16[64,1024]{1,0:T(8,128)(2,1)S(1)}, bf16[64,1024]{1,0:T(8,128)(2,1)}, u32[]{:S(2)}, u32[]{:S(2)}) collective-permute-start(bf16[64,1024]{1,0:T(8,128)(2,1)S(1)} %reshape_squeeze.7), channel_id=1, source_target_pairs={{0,12},{2,14},{4,0},{6,2},{8,4},{10,6},{12,8},{14,10},{1,13},{3,15... | collective-permute-start | bytes 393224 | tf_op jit(solution)/shard_map/ppermute | solution.py:306
  5.9 11.1 %collective-permute-start.14 = (bf16[64,1024]{1,0:T(8,128)(2,1)S(1)}, bf16[64,1024]{1,0:T(8,128)(2,1)S(1)}, u32[]{:S(2)}, u32[]{:S(2)}) collective-permute-start(bf16[64,1024]{1,0:T(8,128)(2,1)S(1)} %reshape_squeeze.7), channel_id=1, source_target_pairs={{0,4},{2,6},{4,8},{6,10},{8,12},{10,14},{12,0},{14,2},{1,5},{3,7},... | collective-permute-start | bytes 393224 | tf_op jit(solution)/shard_map/ppermute | solution.py:306
  7.7 6.3 %collective-permute-start.18 = (bf16[64,1024]{1,0:T(8,128)(2,1)S(1)}, bf16[64,1024]{1,0:T(8,128)(2,1)S(1)}, u32[]{:S(2)}, u32[]{:S(2)}) collective-permute-start(bf16[64,1024]{1,0:T(8,128)(2,1)S(1)} %reshape_squeeze.6.q_ref), channel_id=1, source_target_pairs={{0,64},{16,80},{32,96},{48,112},{64,0},{80,16},{96,32},{112,48},{1... | collective-permute-start | bytes 393224 | tf_op jit(solution)/shard_map/ppermute | solution.py:298
  9.7 29.3 %copy-start.7 = (s32[2,16]{1,0:T(2,128)S(1)}, s32[2,16]{1,0:T(2,128)}, u32[]{:S(2)}) copy-start(s32[2,16]{1,0:T(2,128)} %param.16) | copy-start | bytes 388
  10.7 9.3 %collective-permute-start.9 = (bf16[256,256]{1,0:T(8,128)(2,1)S(1)}, bf16[256,256]{1,0:T(8,128)(2,1)S(1)}, u32[]{:S(2)}, u32[]{:S(2)}) collective-permute-start(bf16[256,256]{1,0:T(8,128)(2,1)S(1)} %get-tuple-element.14), channel_id=1, source_target_pairs={{0,192},{16,208},{32,224},{48,240},{64,128},{80,144},{96,160},{112... | collective-permute-start | bytes 393224 | tf_op jit(solution)/shard_map/ppermute | solution.py:298
  14.0 7.3 %collective-permute-start.4 = (bf16[256,256]{1,0:T(8,128)(2,1)S(1)}, bf16[256,256]{1,0:T(8,128)(2,1)S(1)}, u32[]{:S(2)}, u32[]{:S(2)}) collective-permute-start(bf16[256,256]{1,0:T(8,128)(2,1)S(1)} %get-tuple-element.14), channel_id=1, source_target_pairs={{0,64},{16,80},{32,96},{48,112},{64,0},{80,16},{96,32},{112,48},{1... | collective-permute-start | bytes 393224 | tf_op jit(solution)/shard_map/ppermute | solution.py:298
  16.3 6.0 %collective-permute-start.8 = (bf16[256,256]{1,0:T(8,128)(2,1)S(1)}, bf16[256,256]{1,0:T(8,128)(2,1)S(1)}, u32[]{:S(2)}, u32[]{:S(2)}) collective-permute-start(bf16[256,256]{1,0:T(8,128)(2,1)S(1)} %get-tuple-element.15.refs_0_), channel_id=1, source_target_pairs={{0,128},{16,144},{32,160},{48,176},{64,192},{80,208},{96,224},{112... | collective-permute-start | bytes 393224 | tf_op jit(solution)/shard_map/ppermute | solution.py:298
  16.5 7.9 %collective-permute-start.3 = (bf16[256,256]{1,0:T(8,128)(2,1)S(1)}, bf16[256,256]{1,0:T(8,128)(2,1)S(1)}, u32[]{:S(2)}, u32[]{:S(2)}) collective-permute-start(bf16[256,256]{1,0:T(8,128)(2,1)S(1)} %get-tuple-element.15.refs_0_), channel_id=1, source_target_pairs={{0,32},{16,48},{32,0},{48,16},{64,96},{80,112},{96,64},{112,80},{1... | collective-permute-start | bytes 393224 | tf_op jit(solution)/shard_map/ppermute | solution.py:294
  17.0 8.6 %copy-start.6 = (bf16[64,1024]{1,0:T(8,128)(2,1)}, bf16[64,1024]{1,0:T(8,128)(2,1)S(1)}, u32[]{:S(2)}) copy-start(bf16[64,1024]{1,0:T(8,128)(2,1)S(1)} %collective-permute-done.14) | copy-start | bytes 393220
  17.0 8.6 %collective-permute-start.2 = (bf16[256,256]{1,0:T(8,128)(2,1)S(1)}, bf16[256,256]{1,0:T(8,128)(2,1)S(1)}, u32[]{:S(2)}, u32[]{:S(2)}) collective-permute-start(bf16[256,256]{1,0:T(8,128)(2,1)S(1)} %get-tuple-element.15.refs_0_), channel_id=1, source_target_pairs={{0,48},{16,0},{32,16},{48,32},{64,112},{80,64},{96,80},{112,96},{1... | collective-permute-start | bytes 393224 | tf_op jit(solution)/shard_map/ppermute | solution.py:294
  20.1 7.6 %collective-permute-start.1 = (bf16[256,256]{1,0:T(8,128)(2,1)S(1)}, bf16[256,256]{1,0:T(8,128)(2,1)S(1)}, u32[]{:S(2)}, u32[]{:S(2)}) collective-permute-start(bf16[256,256]{1,0:T(8,128)(2,1)S(1)} %get-tuple-element.15.refs_0_), channel_id=1, source_target_pairs={{0,16},{16,32},{32,48},{48,0},{64,80},{80,96},{96,112},{112,64},{1... | collective-permute-start | bytes 393224 | tf_op jit(solution)/shard_map/ppermute | solution.py:294
  21.3 7.7 %collective-permute-start.7 = (bf16[256,256]{1,0:T(8,128)(2,1)S(1)}, bf16[256,256]{1,0:T(8,128)(2,1)S(1)}, u32[]{:S(2)}, u32[]{:S(2)}) collective-permute-start(bf16[256,256]{1,0:T(8,128)(2,1)S(1)} %collective-permute-done.4.refs_4_), channel_id=1, source_target_pairs={{0,32},{16,48},{32,0},{48,16},{64,96},{80,112},{96,64},{112,80},{1... | collective-permute-start | bytes 393224 | tf_op jit(solution)/shard_map/ppermute | solution.py:294
  22.4 9.3 %collective-permute-start.6 = (bf16[256,256]{1,0:T(8,128)(2,1)S(1)}, bf16[256,256]{1,0:T(8,128)(2,1)S(1)}, u32[]{:S(2)}, u32[]{:S(2)}) collective-permute-start(bf16[256,256]{1,0:T(8,128)(2,1)S(1)} %collective-permute-done.4.refs_4_), channel_id=1, source_target_pairs={{0,48},{16,0},{32,16},{48,32},{64,112},{80,64},{96,80},{112,96},{1... | collective-permute-start | bytes 393224 | tf_op jit(solution)/shard_map/ppermute | solution.py:294
  24.4 7.3 %collective-permute-start.5 = (bf16[256,256]{1,0:T(8,128)(2,1)S(1)}, bf16[256,256]{1,0:T(8,128)(2,1)S(1)}, u32[]{:S(2)}, u32[]{:S(2)}) collective-permute-start(bf16[256,256]{1,0:T(8,128)(2,1)S(1)} %collective-permute-done.4.refs_4_), channel_id=1, source_target_pairs={{0,16},{16,32},{32,48},{48,0},{64,80},{80,96},{96,112},{112,64},{1... | collective-permute-start | bytes 393224 | tf_op jit(solution)/shard_map/ppermute | solution.py:294
  25.6 37.1 %collective-permute-start = (bf16[256,1024]{1,0:T(8,128)(2,1)}, bf16[256,1024]{1,0:T(8,128)(2,1)S(1)}, u32[]{:S(2)}, u32[]{:S(2)}) collective-permute-start(bf16[256,1024]{1,0:T(8,128)(2,1)} %get-tuple-element.11), channel_id=1, source_target_pairs={{0,64},{16,80},{32,96},{48,112},{64,0},{80,16},{96,32},{112,48},{1... | collective-permute-start | bytes 1572872 | tf_op jit(solution)/shard_map/ppermute | solution.py:298
  27.7 16.0 %collective-permute-start.12 = (bf16[2,256,256]{2,1,0:T(8,128)(2,1)S(1)}, bf16[2,256,256]{2,1,0:T(8,128)(2,1)S(1)}, u32[]{:S(2)}, u32[]{:S(2)}) collective-permute-start(bf16[2,256,256]{2,1,0:T(8,128)(2,1)S(1)} %pad_maximum_fusion.1.refs_0_.refs_8_), channel_id=1, source_target_pairs={{0,32},{16,48},{32,0},{48,16},{64,96},{80,112},{96,64},{112,80},{1... | collective-permute-start | bytes 786440 | tf_op jit(solution)/shard_map/ppermute | solution.py:294
  29.0 14.8 %collective-permute-start.11 = (bf16[2,256,256]{2,1,0:T(8,128)(2,1)S(1)}, bf16[2,256,256]{2,1,0:T(8,128)(2,1)S(1)}, u32[]{:S(2)}, u32[]{:S(2)}) collective-permute-start(bf16[2,256,256]{2,1,0:T(8,128)(2,1)S(1)} %pad_maximum_fusion.1.refs_0_.refs_8_), channel_id=1, source_target_pairs={{0,48},{16,0},{32,16},{48,32},{64,112},{80,64},{96,80},{112,96},{1... | collective-permute-start | bytes 786440 | tf_op jit(solution)/shard_map/ppermute | solution.py:294
  31.7 12.2 %collective-permute-start.10 = (bf16[2,256,256]{2,1,0:T(8,128)(2,1)S(1)}, bf16[2,256,256]{2,1,0:T(8,128)(2,1)S(1)}, u32[]{:S(2)}, u32[]{:S(2)}) collective-permute-start(bf16[2,256,256]{2,1,0:T(8,128)(2,1)S(1)} %pad_maximum_fusion.1.refs_0_.refs_8_), channel_id=1, source_target_pairs={{0,16},{16,32},{32,48},{48,0},{64,80},{80,96},{96,112},{112,64},{1... | collective-permute-start | bytes 786440 | tf_op jit(solution)/shard_map/ppermute | solution.py:294
  31.7 0.7 copy-start.3
  32.3 22.2 %collective-permute-start.19 = (bf16[2,64,1024]{2,1,0:T(8,128)(2,1)}, bf16[2,64,1024]{2,1,0:T(8,128)(2,1)S(1)}, u32[]{:S(2)}, u32[]{:S(2)}) collective-permute-start(bf16[2,64,1024]{2,1,0:T(8,128)(2,1)} %pad_maximum_fusion.2), channel_id=1, source_target_pairs={{0,1},{1,0},{16,17},{17,16},{32,33},{33,32},{48,49},{49,48},{64,65... | collective-permute-start | bytes 786440 | tf_op jit(solution)/shard_map/ppermute | solution.py:311
  43.7 51.7 %collective-permute-start.17 = (bf16[4,64,1024]{2,1,0:T(8,128)(2,1)S(1)}, bf16[4,64,1024]{2,1,0:T(8,128)(2,1)S(1)}, u32[]{:S(2)}, u32[]{:S(2)}) collective-permute-start(bf16[4,64,1024]{2,1,0:T(8,128)(2,1)S(1)} %pad_maximum_fusion.near_ref), channel_id=1, source_target_pairs={{0,2},{2,0},{4,6},{6,4},{8,10},{10,8},{12,14},{14,12},{1,3},{3,1},... | collective-permute-start | bytes 1572872 | tf_op jit(solution)/shard_map/ppermute | solution.py:364
  54.5 0.9 copy-start.4
  81.0 20.0 %collective-permute-start.13 = (bf16[256,1024]{1,0:T(8,128)(2,1)S(1)}, bf16[256,1024]{1,0:T(8,128)(2,1)S(1)}, u32[]{:S(2)}, u32[]{:S(2)}) collective-permute-start(bf16[256,1024]{1,0:T(8,128)(2,1)S(1)} %shard_map.106), channel_id=1, source_target_pairs={{0,64},{16,80},{32,96},{48,112},{64,0},{80,16},{96,32},{112,48},{1... | collective-permute-start | bytes 1572872 | tf_op jit(solution)/shard_map/ppermute | solution.py:298
  81.1 18.4 %collective-permute-start.21 = (bf16[64,1152]{1,0:T(8,128)(2,1)S(1)}, bf16[64,1152]{1,0:T(8,128)(2,1)S(1)}, u32[]{:S(2)}, u32[]{:S(2)}) collective-permute-start(bf16[64,1152]{1,0:T(8,128)(2,1)S(1)} %get-tuple-element.12), channel_id=1, source_target_pairs={{0,65},{1,64},{16,81},{17,80},{32,97},{33,96},{48,113},{49,112},{6... | collective-permute-start | bytes 442376 | tf_op jit(solution)/shard_map/ppermute | solution.py:311
  82.3 13.1 %copy-start = (bf16[8192,256]{1,0:T(8,128)(2,1)S(1)}, bf16[8192,256]{1,0:T(8,128)(2,1)}, u32[]{:S(2)}) copy-start(bf16[8192,256]{1,0:T(8,128)(2,1)} %weight_ref.1) | copy-start | bytes 12582916
  82.3 13.1 %copy-start.1 = (bf16[1,1,16,256,256]{4,3,2,1,0:T(8,128)(2,1)S(1)}, bf16[1,1,16,256,256]{4,3,2,1,0:T(8,128)(2,1)}, u32[]{:S(2)}) copy-start(bf16[1,1,16,256,256]{4,3,2,1,0:T(8,128)(2,1)} %param.12) | copy-start | bytes 6291460
  82.3 17.2 %collective-permute-start.20 = (bf16[64,1152]{1,0:T(8,128)(2,1)S(1)}, bf16[64,1152]{1,0:T(8,128)(2,1)S(1)}, u32[]{:S(2)}, u32[]{:S(2)}) collective-permute-start(bf16[64,1152]{1,0:T(8,128)(2,1)S(1)} %get-tuple-element.13), channel_id=1, source_target_pairs={{0,1},{1,0},{16,17},{17,16},{32,33},{33,32},{48,49},{49,48},{64,65... | collective-permute-start | bytes 442376 | tf_op jit(solution)/shard_map/ppermute | solution.py:311

commit v3 on v2

v3 whole, which is shorter than its diff:
```python
import functools

import jax
import jax.numpy as jnp
from jax import lax
from jax.experimental import pallas as pl
from jax.experimental.pallas import tpu as pltpu
from jax.sharding import PartitionSpec as P

D = 8192
HD = 128
GROUP = 8
BLOCK = 256
DECODE_ROWS = 64
MASKED = -1e30
LOG2E = 1.4426950408889634
SCALE2 = HD ** (-0.5) * LOG2E
MIB = 1024 * 1024

bf16 = jnp.bfloat16
f32 = jnp.float32


def scores_of(rows, keys):
    return lax.dot_general(rows, keys, (((1,), (1,)), ((), ())), preferred_element_type=f32)


def place():
    index = lax.axis_index("ctx")
    return index // 4, index % 4, index // 4 % 2


def fill_values(aug_ref, index, block):
    aug_ref[index, :, :HD] = block[:, HD:]
    aug_ref[index, :, HD:] = jnp.ones((BLOCK, HD), bf16)


def weigh(parts, highest, aug_blocks):
    out = None
    for part, aug in zip(parts, aug_blocks):
        weights = jnp.exp2((part - highest) * SCALE2).astype(bf16)
        term = jnp.dot(weights, aug, preferred_element_type=f32)
        out = term if out is None else out + term
    return out


def max_of(parts):
    top = parts[0]
    for part in parts[1:]:
        top = jnp.maximum(top, part)
    return jnp.max(top, axis=-1, keepdims=True)


def flatten(target_ref, source_ref):
    for s in range(16):
        target_ref[s * 4 : s * 4 + 4] = source_ref[s]


def first_kernel(own_q, partner_q, hidden_in, rows_in, *refs):
    blocks = refs[:4]
    acc_ref, stat_ref, hidden_ref, rows_ref, aug_scr = refs[4:]
    flatten(hidden_ref, hidden_in)
    flatten(rows_ref, rows_in)
    _, row_y, parity = place()
    for group in range(2):
        for b in range(4):
            fill_values(aug_scr, group * 4 + b, blocks[b][group])
    lane = lax.broadcasted_iota(jnp.int32, (BLOCK, HD), 1)
    upper = lax.broadcasted_iota(jnp.int32, (BLOCK, BLOCK), 1) > lax.broadcasted_iota(
        jnp.int32, (BLOCK, BLOCK), 0
    )

    def shift_of(b):
        block_y = (row_y + (0, 3, 1, 2)[b]) % 4
        return jnp.where(block_y < row_y, 0.0, MASKED).astype(f32)

    for odd in (True, False):
        side = 1 - parity if odd else parity
        same = side * 4
        other = (1 - side) * 4

        def head(h, carry):
            at = pl.ds(pl.multiple_of(h * HD, HD), HD)
            rows = jnp.where(side == 0, own_q[parity, :, at], partner_q[:, at])
            parts = []
            augs = []
            for b in range(4):
                part = scores_of(rows, blocks[b][side, :, :HD])
                if b == 0:
                    part = jnp.where(upper, MASKED, part)
                else:
                    part = part + shift_of(b)
                parts.append(part)
                augs.append(aug_scr[same + b])
            if odd:
                for b in range(4):
                    parts.append(scores_of(rows, blocks[b][1 - side, :, :HD]))
                    augs.append(aug_scr[other + b])
            highest = max_of(parts)
            mixed = weigh(parts, highest, augs)
            acc_ref[side, h] = mixed[:, :HD]
            old = jnp.where(lane == h, highest, stat_ref[side])
            stat_ref[side] = jnp.where(lane == h + 8, mixed[:, HD:], old)
            return carry

        lax.fori_loop(0, GROUP, head, 0, unroll=4)


def last_kernel(own, q_ref, acc_ref, stat_ref, *refs):
    kv_refs = refs[:4]
    out_ref, extra_ref, aug_scr, out_scr, sems = refs[-5:]
    if own:
        extra_ref[...] = jnp.zeros_like(extra_ref)
    else:
        extra_ref[0] = refs[4][...]
        extra_ref[1] = refs[5][...]
    z, _, parity = place()
    side = 0 if own else 1
    if own:
        q_ref = q_ref.at[parity]
        out_ref = out_ref.at[parity]
    lane = lax.broadcasted_iota(jnp.int32, (BLOCK, HD), 1)

    def column(h):
        return jnp.sum(jnp.where(lane == h, stat_ref[side], 0.0), axis=-1, keepdims=True)

    def copy_of(half):
        at = pl.ds(pl.multiple_of(half * 4 * HD, 4 * HD), 4 * HD)
        return pltpu.make_async_copy(out_scr.at[:, at], out_ref.at[:, at], sems.at[half])

    def halves(head):
        def step(half, carry):
            for i in range(4):
                head(half * 4 + i)
            copy_of(half).start()
            return carry

        lax.fori_loop(0, 2, step, 0)

    @pl.when(z >= 2)
    def _():
        for b in range(8):
            fill_values(aug_scr, b, kv_refs[b // 2][b % 2])

        def head(h):
            at = pl.ds(pl.multiple_of(h * HD, HD), HD)
            rows = q_ref[:, at]
            parts = [scores_of(rows, kv_refs[b // 2][b % 2, :, :HD]) for b in range(8)]
            before = column(h)
            highest = jnp.maximum(before, max_of(parts))
            mixed = weigh(parts, highest, [aug_scr[b] for b in range(8)])
            fade = jnp.exp2((before - highest) * SCALE2)
            total = column(h + 8) * fade + mixed[:, HD:]
            out_scr[:, at] = ((acc_ref[side, h] * fade + mixed[:, :HD]) / total).astype(bf16)

        halves(head)

    @pl.when(z < 2)
    def _():
        def head(h):
            at = pl.ds(pl.multiple_of(h * HD, HD), HD)
            out_scr[:, at] = (acc_ref[side, h] / column(h + 8)).astype(bf16)

        halves(head)

    for half in range(2):
        copy_of(half).wait()


def segment_kernel(prompt_ref, _, rows0_ref, rows1_ref, *refs):
    kv_refs = refs[:8]
    out0_ref, out1_ref, done_ref, aug_scr = refs[-4:]
    done_ref[...] = jnp.zeros_like(done_ref)
    index, pool = lax.axis_index("ctx"), lax.axis_index("pd")
    parity = place()[2]

    def block_of(b, at):
        return kv_refs[b // 2][b % 2, :, at]

    for b in range(16):
        aug_scr[b, :, :HD] = block_of(b, slice(HD, 2 * HD))
        aug_scr[b, :, HD:] = jnp.ones((BLOCK, HD), bf16)
    lane = lax.broadcasted_iota(jnp.int32, (DECODE_ROWS, HD), 1)

    for which, rows_ref, out_ref in ((0, rows0_ref, out0_ref), (1, rows1_ref, out1_ref)):
        needed = prompt_ref[pool, index ^ (4 * which)] == parity

        @pl.when(needed)
        def _():
            stat = jnp.zeros((DECODE_ROWS, HD), f32)
            for tile in range(2):
                heads = range(tile * 4, tile * 4 + 4)
                rows = jnp.concatenate(
                    [rows_ref[:, h * HD : (h + 1) * HD] for h in heads], axis=0
                )
                highest = None
                for chunk in range(4):
                    blocks = range(chunk * 4, chunk * 4 + 4)
                    parts = [scores_of(rows, block_of(b, slice(0, HD))) for b in blocks]
                    top = max_of(parts)
                    if highest is None:
                        mixed = weigh(parts, top, [aug_scr[b] for b in blocks])
                    else:
                        top = jnp.maximum(top, highest)
                        mixed = mixed * jnp.exp2((highest - top) * SCALE2) + weigh(
                            parts, top, [aug_scr[b] for b in blocks]
                        )
                    highest = top
                total = mixed[:, HD:]
                share = (mixed[:, :HD] / total).astype(bf16)
                level = highest * SCALE2 + jnp.log2(total)
                for i, h in enumerate(heads):
                    at = slice(i * DECODE_ROWS, (i + 1) * DECODE_ROWS)
                    out_ref[:, h * HD : (h + 1) * HD] = share[at]
                    stat = jnp.where(lane == h, level[at], stat)
            high = stat.astype(bf16).astype(f32)
            middle = (stat - high).astype(bf16).astype(f32)
            low = stat - high - middle
            pieces = high + pltpu.roll(middle, 8, 1) + pltpu.roll(low, 16, 1)
            out_ref[:, GROUP * HD :] = pieces.astype(bf16)

        @pl.when(jnp.logical_not(needed))
        def _():
            out_ref[...] = jnp.zeros_like(out_ref)


def local_kernel(
    len_ref, _, cos_ref, sin_ref, gain_ref, q_ref, own_ref, twin_ref, *refs
):
    pairs = refs[:3]
    weight_ref, cache_ref = refs[3:5]
    out_ref, level_ref = refs[-2:]
    width = own_ref.shape[1]
    core, x = lax.axis_index("tp") % 2, lax.axis_index("tp") // 2
    squares = jnp.zeros((DECODE_ROWS, 1), f32)
    projected = jnp.zeros((DECODE_ROWS, 2 * HD), f32)
    for i, step in enumerate((0, 3, 1, 2)):
        for side in range(2):
            owner = ((x + step) % 4) * 2 + (core if side == 0 else 1 - core)
            if i == 0:
                wide = (own_ref, twin_ref)[side][...].astype(f32)
            else:
                wide = pairs[i - 1][side].astype(f32)
            at = pl.ds(pl.multiple_of(owner * width, width), width)
            squares = squares + jnp.sum(wide * wide, axis=-1, keepdims=True)
            scaled = (wide * gain_ref[:, at]).astype(bf16)
            projected = projected + jnp.dot(
                scaled, weight_ref[at], preferred_element_type=f32
            )
    normed = projected * lax.rsqrt(squares / D + 1e-6)
    key_rows = normed[:, :HD]
    turned = pltpu.roll(key_rows, HD // 2, 1)
    fresh_k = (key_rows * cos_ref[...] + turned * sin_ref[...]).astype(bf16)
    fresh_v = normed[:, HD:].astype(bf16)
    fresh_aug = jnp.concatenate([fresh_v, jnp.ones((DECODE_ROWS, HD), bf16)], axis=1)
    ones = jnp.ones((BLOCK, HD), bf16)
    row = lax.broadcasted_iota(jnp.int32, (128, BLOCK), 0)
    slot = lax.broadcasted_iota(jnp.int32, (128, BLOCK), 1)
    fresh_row = lax.broadcasted_iota(jnp.int32, (128, DECODE_ROWS), 0) % 16
    fresh_slot = lax.broadcasted_iota(jnp.int32, (128, DECODE_ROWS), 1)

    for g in range(4):
        at = slice(g * 16, (g + 1) * 16)
        rows = jnp.concatenate([q_ref[at, h * HD : (h + 1) * HD] for h in range(GROUP)], axis=0)
        parts = []
        augs = []
        for j in range(4):
            s = g * 4 + j
            allowed = (row % 16 // 4 == j) & (slot < len_ref[s])
            parts.append(jnp.where(allowed, scores_of(rows, cache_ref[s, :, :HD]), MASKED))
            augs.append(jnp.concatenate([cache_ref[s, :, HD:], ones], axis=1))
        behind = fresh_row + g * 16 - fresh_slot
        allowed = (behind >= 0) & (behind <= fresh_row % 4)
        fresh_part = jnp.where(allowed, scores_of(rows, fresh_k), MASKED)
        highest = jnp.maximum(max_of(parts), jnp.max(fresh_part, axis=-1, keepdims=True))
        mixed = weigh(parts + [fresh_part], highest, augs + [fresh_aug])
        total = mixed[:, HD:]
        share = mixed[:, :HD] / total
        level = highest * SCALE2 + jnp.log2(total)
        for h in range(GROUP):
            out_ref[at, h * HD : (h + 1) * HD] = share[h * 16 : (h + 1) * 16]
            level_ref[at, h * HD : (h + 1) * HD] = level[h * 16 : (h + 1) * 16]


def merge_kernel(
    prompt_ref, local_ref, level_ref, same_ref, other_ref, returned_ref, own_out, out_ref, full_ref,
    sem,
):
    del own_out
    parity = place()[2]
    copy = pltpu.make_async_copy(returned_ref, full_ref.at[1 - parity], sem)
    copy.start()
    lane = lax.broadcasted_iota(jnp.int32, (DECODE_ROWS, HD), 1)
    held_here = prompt_ref[1 - lax.axis_index("pd"), lax.axis_index("ctx")] == parity

    def merge(part_ref):
        pieces = part_ref[:, GROUP * HD :].astype(f32)
        for h in range(GROUP):
            at = slice(h * HD, (h + 1) * HD)
            mine = (lane == h) | (lane == h + 8) | (lane == h + 16)
            far = jnp.sum(jnp.where(mine, pieces, 0.0), axis=-1, keepdims=True)
            near = level_ref[:, at]
            top = jnp.maximum(far, near)
            far_share = jnp.exp2(far - top)
            near_share = jnp.exp2(near - top)
            mixed = part_ref[:, at].astype(f32) * far_share + local_ref[:, at] * near_share
            merged = mixed / (far_share + near_share)
            for s in range(16):
                out_ref[s, :, at] = merged[s * 4 : s * 4 + 4].astype(bf16)

    @pl.when(held_here)
    def _():
        merge(same_ref)

    @pl.when(jnp.logical_not(held_here))
    def _():
        merge(other_ref)

    copy.wait()


SMEM = pl.BlockSpec(memory_space=pltpu.SMEM)
VMEM = pl.BlockSpec(memory_space=pltpu.VMEM)
ANY = pl.BlockSpec(memory_space=pl.ANY)


def call(
    kernel, out_shape, args, scalars=0, scratch=(), flops=0, touched=0, exps=0, specs=None,
    out_specs=None, aliases=None, vmem=14,
):
    in_specs = [SMEM] * scalars + [VMEM] * (len(args) - scalars)
    for at, spec in (specs or {}).items():
        in_specs[at] = spec
    return pl.pallas_call(
        kernel,
        out_shape=out_shape,
        in_specs=in_specs,
        out_specs=out_specs or jax.tree.map(lambda _: VMEM, out_shape),
        scratch_shapes=list(scratch),
        input_output_aliases=aliases or {},
        compiler_params=pltpu.CompilerParams(vmem_limit_bytes=vmem * MIB),
        cost_estimate=pl.CostEstimate(flops=flops, bytes_accessed=touched, transcendentals=exps),
    )(*args)


def after(value, *others):
    return lax.optimization_barrier((value, *others))[0]


def y_turn(block, distance):
    route = [(i, i // 4 * 4 + (i % 4 + distance) % 4) for i in range(16)]
    return lax.ppermute(block, "ctx", route)


def z_swap(block, bits):
    return lax.ppermute(block, "ctx", [(i, i ^ (4 * bits)) for i in range(16)])


def y_all(block):
    return [block, y_turn(block, 1), y_turn(block, -1), y_turn(block, 2)]


def tp_turn(block, distance):
    return lax.ppermute(block, "tp", [(i, (i + distance) % 8) for i in range(8)])


def pool_swap(block, z_bits):
    route = [(i, (i ^ 1) ^ (8 * z_bits)) for i in range(32)]
    return lax.ppermute(block, ("ctx", "pd"), route)


def on_device(
    prefill_query,
    prefill_kv,
    decode_query,
    gen_cache,
    new_hidden,
    norm_gain,
    kv_weight,
    prompt_of,
    cached_len,
):
    queries = prefill_query[0]
    keyvals = prefill_kv[0]
    even = lax.axis_index("ctx") // 4 % 2 == 0
    shape = jax.ShapeDtypeStruct

    kv_keep = jnp.where(even, keyvals[0], keyvals[1])
    kv_give = jnp.where(even, keyvals[1], keyvals[0])
    from_z1 = z_swap(kv_give, 1)
    from_z2 = z_swap(kv_keep, 2)
    from_z3 = z_swap(kv_give, 3)
    q_give = lax.dynamic_index_in_dim(queries, even.astype(jnp.int32), 0, keepdims=False)
    samples, steps, width = new_hidden.shape[2:]
    decode_rows = samples * steps
    from_z1, q_give = lax.optimization_barrier((from_z1, q_give))
    first_pair, q_give = lax.optimization_barrier((jnp.stack([kv_keep, from_z1]), q_give))
    group01 = y_all(first_pair)
    q_partner = z_swap(q_give, 1)
    group23 = y_all(jnp.stack([from_z2, from_z3]))

    lengths = cached_len[0, 0]
    half = HD // 2
    frequency = 1000000.0 ** (-jnp.arange(half, dtype=f32) * 2.0 / HD)
    positions = (4096 + lengths[:, None] + jnp.arange(steps, dtype=jnp.int32)[None, :]).astype(f32)
    angles = positions.reshape(-1)[:, None] * frequency
    cosine, sine = jnp.cos(angles), jnp.sin(angles)
    cos_all = jnp.concatenate([cosine, cosine], axis=-1)
    sin_all = jnp.concatenate([-sine, sine], axis=-1)

    token = shape((8, HD), f32)
    flat = shape((decode_rows, width), bf16)
    acc, stat, hidden, step_rows = call(
        first_kernel,
        (shape((2, GROUP, BLOCK, HD), f32), shape((2, BLOCK, HD), f32), flat, flat),
        (queries, q_partner, new_hidden[0, 0], decode_query[0, 0], *group01),
        scratch=(
            pltpu.VMEM((8, BLOCK, 2 * HD), bf16),
        ),
        flops=3 * 2048 * 1024 * 512,
        touched=4 << 20,
        exps=3 * 2048 * 1024,
    )
    twin = lax.ppermute(hidden, "tp", [(i, i ^ 1) for i in range(8)])
    rows_pair = [pool_swap(step_rows, 0), pool_swap(step_rows, 1)]

    def finish(own, q_rows, extra):
        out_rows = (BLOCK, GROUP * HD)
        last = token if own else shape((2, decode_rows, width), bf16)
        return call(
            functools.partial(last_kernel, own),
            (shape((2, *out_rows) if own else out_rows, bf16), last),
            (q_rows, acc, stat, *group23, *extra),
            scratch=(
                pltpu.VMEM((8, BLOCK, 2 * HD), bf16),
                pltpu.VMEM(out_rows, bf16),
                pltpu.SemaphoreType.DMA((2,)),
            ),
            specs={7: ANY} if own else None,
            out_specs=(ANY, VMEM),
            flops=2 * 2048 * 1024 * 512,
            touched=4 << 20,
            exps=2 * 2048 * 1024,
        )

    out_partner, pair = finish(False, q_partner, (hidden, twin))
    returned = z_swap(out_partner, 1)
    pairs = [tp_turn(pair, 2), tp_turn(pair, -2), tp_turn(pair, 4)]
    part = shape((decode_rows, width + HD), bf16)
    segment0, segment1, segment_done = call(
        segment_kernel,
        (part, part, token),
        (prompt_of, pair, *rows_pair, *group01, *group23),
        specs={1: ANY},
        scalars=1,
        scratch=(pltpu.VMEM((16, BLOCK, 2 * HD), bf16),),
        flops=1024 * 4096 * 512,
        touched=3 << 20,
        exps=1024 * 4096,
    )
    back0 = pool_swap(segment0, 0)
    back1 = pool_swap(segment1, 1)
    out_own, own_done = finish(True, queries, (segment_done,))
    local_out, local_level = call(
        local_kernel,
        (shape((decode_rows, width), f32), shape((decode_rows, width), f32)),
        (
            lengths,
            own_done,
            cos_all,
            sin_all,
            norm_gain[None],
            step_rows,
            hidden,
            twin,
            *pairs,
            kv_weight,
            gen_cache[0, 0],
        ),
        scalars=1,
        specs={1: ANY},
        flops=2 * 64 * D * 256,
        touched=8 << 20,
        exps=512 * 320,
    )

    merged, segment_out = call(
        merge_kernel,
        (shape((samples, steps, width), bf16), shape(queries.shape, bf16)),
        (prompt_of, local_out, local_level, back0, back1, returned, out_own),
        scalars=1,
        scratch=(pltpu.SemaphoreType.DMA,),
        flops=512 * HD * 8,
        touched=1 << 20,
        exps=512 * HD * 2,
        specs={5: ANY, 6: ANY},
        out_specs=(VMEM, ANY),
        aliases={6: 1},
        vmem=8,
    )
    return (segment_out[None], merged[None, None])


def solution(mesh):
    placed = (
        P("pd", None, "ctx", "tp"),
        P("pd", None, "ctx", "tp"),
        P("pd", "ctx", None, None, "tp"),
        P("pd", "ctx", None, None, "tp"),
        P("pd", "ctx", None, None, "tp"),
        P(),
        P(None, "tp"),
        P(),
        P("pd", "ctx", None),
    )
    return jax.shard_map(
        on_device,
        mesh=mesh,
        in_specs=placed,
        out_specs=(P("pd", None, "ctx", "tp"), P("pd", "ctx", None, None, "tp")),
        check_vma=False,
    )
```

time: 103 us -> 84.2 us (0.82)
  the two profiles are of different devices: /device:TPU:80 before, /device:TPU:70 now
where the time goes in v3:
time: 84.2 us; the launch traced here: 83.1 us
  starting transfers between devices  39.4 us (47%)
  Pallas kernels  31.7 us (38%)
  waiting for transfers between devices  7.22 us (9%)
  other arithmetic  2.47 us (3%)
  local copies, waits for them, and re-layouts  1.2 us (1%)
  between operations  1.08 us (1%)
    pallas_call x6, Pallas kernels, call(): pl.pallas_call(kernel, out_shape=out_shape, in_specs=in_specs, out_specs=...  31.7 us
    ppermute x4, starting transfers between devices, pool_swap(): return lax.ppermute(block, ('ctx', 'pd'), route)  12.5 us
    ppermute x5, starting transfers between devices, z_swap(): return lax.ppermute(block, 'ctx', [(i, i ^ 4 * bits) for i in range(16)])  12.3 us
    ppermute x6, starting transfers between devices, y_turn(): return lax.ppermute(block, 'ctx', route)  10.7 us
    ppermute x6, waiting for transfers between devices, y_turn(): return lax.ppermute(block, 'ctx', route)  5.29 us
    ppermute x3, starting transfers between devices, tp_turn(): lax.ppermute(block, 'tp', [(i, (i + distance) % 8) for i in range(8)])  3.58 us
    ppermute x5, waiting for transfers between devices, z_swap(): return lax.ppermute(block, 'ctx', [(i, i ^ 4 * bits) for i in range(16)])  1.91 us
  transfers between devices with their start and end apart: 19, of which 3 were waited for; matrix products, arithmetic and copies ran while one was open for 3% of the time, Pallas kernels for 36%

profile of v3, /device:TPU:70, one launch (start us, length us, event | category | flops | bytes accessed | tf_op | source)
XLA Modules:
  0.0 83.1 jit_solution(12173749787042990393)
XLA Ops:
  0.7 1.1 %fusion = (bf16[256,256]{1,0:T(8,128)(2,1)S(1)}, bf16[1,256,256]{2,1,0:T(8,128)(2,1)S(1)}, bf16[256,256]{1,0:T(8,128)(2,1)S(1)}) fusion(bf16[1,2,256,256]{3,2,1,0:T(8,128)(2,1)} %param.10, pred[]{:T(512)S(6)} %eq.5), kind=kLoop, calls=%fused_computation.9 | loop fusion | flops 131072 | bytes 655361 | tf_op jit(solution)/shard_map/jit(_where)/select_n | solution.py:388
  1.8 2.0 %collective-permute-start = (bf16[256,256]{1,0:T(8,128)(2,1)S(1)}, bf16[256,256]{1,0:T(8,128)(2,1)S(1)}, u32[]{:S(2)}, u32[]{:S(2)}) collective-permute-start(bf16[256,256]{1,0:T(8,128)(2,1)S(1)} %get-tuple-element.42), channel_id=1, source_target_pairs={{0,64},{16,80},{32,96},{48,112},{64,0},{80,16},{96,32},{112,48},{1... | collective-permute-start | bytes 393224 | tf_op jit(solution)/shard_map/ppermute | solution.py:356
  3.8 2.5 %collective-permute-start.5 = (bf16[256,256]{1,0:T(8,128)(2,1)S(1)}, bf16[256,256]{1,0:T(8,128)(2,1)}, u32[]{:S(2)}, u32[]{:S(2)}) collective-permute-start(bf16[256,256]{1,0:T(8,128)(2,1)S(1)} %get-tuple-element.40), channel_id=1, source_target_pairs={{0,128},{16,144},{32,160},{48,176},{64,192},{80,208},{96,224},{112... | collective-permute-start | bytes 393224 | tf_op jit(solution)/shard_map/ppermute | solution.py:356
  6.3 1.1 %dynamic-slice_bitcast_fusion = bf16[256,1024]{1,0:T(8,128)(2,1)S(1)} fusion(bf16[1,2,256,1024]{3,2,1,0:T(8,128)(2,1)} %param.9, s32[]{:T(128)S(6)} %select_n.50), kind=kLoop, calls=%fused_computation | loop fusion | bytes 1048580 | tf_op jit(solution)/shard_map/jit(dynamic_index_in_dim)/squeeze | solution.py:393
  7.4 1.9 %collective-permute-done = bf16[256,256]{1,0:T(8,128)(2,1)S(1)} collective-permute-done((bf16[256,256]{1,0:T(8,128)(2,1)S(1)}, bf16[256,256]{1,0:T(8,128)(2,1)S(1)}, u32[]{:S(2)}, u32[]{:S(2)}) %collective-permute-start) | collective-permute-done | bytes 131104 | tf_op jit(solution)/shard_map/ppermute | solution.py:356
  9.3 3.0 %collective-permute-start.1 = (bf16[256,1024]{1,0:T(8,128)(2,1)S(1)}, bf16[256,1024]{1,0:T(8,128)(2,1)S(1)}, u32[]{:S(2)}, u32[]{:S(2)}) collective-permute-start(bf16[256,1024]{1,0:T(8,128)(2,1)S(1)} %dynamic-slice_bitcast_fusion), channel_id=1, source_target_pairs={{0,64},{16,80},{32,96},{48,112},{64,0},{80,16},{96,32},{112,48},{1... | collective-permute-start | bytes 1572872 | tf_op jit(solution)/shard_map/ppermute | solution.py:356
  12.3 1.6 %collective-permute-start.2 = (bf16[2,256,256]{2,1,0:T(8,128)(2,1)S(1)}, bf16[2,256,256]{2,1,0:T(8,128)(2,1)S(1)}, u32[]{:S(2)}, u32[]{:S(2)}) collective-permute-start(bf16[2,256,256]{2,1,0:T(8,128)(2,1)S(1)} %pad_maximum_fusion.refs_0_), channel_id=1, source_target_pairs={{0,16},{16,32},{32,48},{48,0},{64,80},{80,96},{96,112},{112,64},{1... | collective-permute-start | bytes 786440 | tf_op jit(solution)/shard_map/ppermute | solution.py:352
  13.9 1.7 %collective-permute-start.3 = (bf16[2,256,256]{2,1,0:T(8,128)(2,1)S(1)}, bf16[2,256,256]{2,1,0:T(8,128)(2,1)S(1)}, u32[]{:S(2)}, u32[]{:S(2)}) collective-permute-start(bf16[2,256,256]{2,1,0:T(8,128)(2,1)S(1)} %pad_maximum_fusion.refs_0_), channel_id=1, source_target_pairs={{0,48},{16,0},{32,16},{48,32},{64,112},{80,64},{96,80},{112,96},{1... | collective-permute-start | bytes 786440 | tf_op jit(solution)/shard_map/ppermute | solution.py:352
  15.6 3.0 %collective-permute-start.4 = (bf16[2,256,256]{2,1,0:T(8,128)(2,1)S(1)}, bf16[2,256,256]{2,1,0:T(8,128)(2,1)S(1)}, u32[]{:S(2)}, u32[]{:S(2)}) collective-permute-start(bf16[2,256,256]{2,1,0:T(8,128)(2,1)S(1)} %pad_maximum_fusion.refs_0_), channel_id=1, source_target_pairs={{0,32},{16,48},{32,0},{48,16},{64,96},{80,112},{96,64},{112,80},{1... | collective-permute-start | bytes 786440 | tf_op jit(solution)/shard_map/ppermute | solution.py:352
  18.6 0.1 convert_element_type.15
  18.7 1.0 %pad_maximum_fusion.1.refs_0_.refs_4_ = bf16[2,256,256]{2,1,0:T(8,128)(2,1)S(1)} fusion(bf16[1,256,256]{2,1,0:T(8,128)(2,1)} %bitcast.10, bf16[1,256,256]{2,1,0:T(8,128)(2,1)} %bitcast.9), kind=kLoop, calls=%fused_computation.2 | loop fusion | flops 131072 | bytes 524288 | tf_op jit(solution)/shard_map/stack | solution.py:400
  19.7 0.8 collective-permute-start.7
  20.5 2.5 %collective-permute-done.2.refs_1_ = bf16[2,256,256]{2,1,0:T(8,128)(2,1)S(1)} collective-permute-done((bf16[2,256,256]{2,1,0:T(8,128)(2,1)S(1)}, bf16[2,256,256]{2,1,0:T(8,128)(2,1)S(1)}, u32[]{:S(2)}, u32[]{:S(2)}) %collective-permute-start.2) | collective-permute-done | bytes 262176 | tf_op jit(solution)/shard_map/ppermute | solution.py:352
  23.0 1.5 %collective-permute-start.8 = (bf16[2,256,256]{2,1,0:T(8,128)(2,1)S(1)}, bf16[2,256,256]{2,1,0:T(8,128)(2,1)S(1)}, u32[]{:S(2)}, u32[]{:S(2)}) collective-permute-start(bf16[2,256,256]{2,1,0:T(8,128)(2,1)S(1)} %pad_maximum_fusion.1.refs_0_.refs_4_), channel_id=1, source_target_pairs={{0,48},{16,0},{32,16},{48,32},{64,112},{80,64},{96,80},{112,96},{1... | collective-permute-start | bytes 786440 | tf_op jit(solution)/shard_map/ppermute | solution.py:352
  24.4 2.3 %collective-permute-start.9 = (bf16[2,256,256]{2,1,0:T(8,128)(2,1)S(1)}, bf16[2,256,256]{2,1,0:T(8,128)(2,1)S(1)}, u32[]{:S(2)}, u32[]{:S(2)}) collective-permute-start(bf16[2,256,256]{2,1,0:T(8,128)(2,1)S(1)} %pad_maximum_fusion.1.refs_0_.refs_4_), channel_id=1, source_target_pairs={{0,32},{16,48},{32,0},{48,16},{64,96},{80,112},{96,64},{112,80},{1... | collective-permute-start | bytes 786440 | tf_op jit(solution)/shard_map/ppermute | solution.py:352
  26.8 2.8 %collective-permute-done.4.refs_3_ = bf16[2,256,256]{2,1,0:T(8,128)(2,1)S(1)} collective-permute-done((bf16[2,256,256]{2,1,0:T(8,128)(2,1)S(1)}, bf16[2,256,256]{2,1,0:T(8,128)(2,1)S(1)}, u32[]{:S(2)}, u32[]{:S(2)}) %collective-permute-start.4) | collective-permute-done | bytes 262176 | tf_op jit(solution)/shard_map/ppermute | solution.py:352
  29.6 10.3 %shard_map.104 = (f32[2,8,256,128]{3,2,1,0:T(8,128)S(1)}, f32[2,256,128]{2,1,0:T(8,128)S(1)}, bf16[64,1024]{1,0:T(8,128)(2,1)S(1)}, bf16[64,1024]{1,0:T(8,128)(2,1)S(1)}) custom-call(bf16[2,256,1024]{2,1,0:T(8,128)(2,1)S(1)} %bitcast.21, bf16[256,1024]{1,0:T(8,128)(2,1)S(1)} %collective-permute-done.1.partner_q.q_ref, bf16[16,4,1024]{2,1,0:T(4,128)(2,1)S(1)} %bitcast.25, ...), custom_call_target="tpu_custom_call" | custom-call | flops 3221225472 | bytes 4194304 | tf_op jit(solution)/shard_map/pallas_call | solution.py:334
  39.9 0.3 collective-permute-start.10
  40.2 0.2 fusion.2
  40.4 1.8 %collective-permute-start.11 = (bf16[64,1024]{1,0:T(8,128)(2,1)S(1)}, bf16[64,1024]{1,0:T(8,128)(2,1)S(1)}, u32[]{:S(2)}, u32[]{:S(2)}) collective-permute-start(bf16[64,1024]{1,0:T(8,128)(2,1)S(1)} %get-tuple-element.29.q_ref), channel_id=1, source_target_pairs={{0,1},{1,0},{16,17},{17,16},{32,33},{33,32},{48,49},{49,48},{64,65... | collective-permute-start | bytes 393224 | tf_op jit(solution)/shard_map/ppermute | solution.py:369
  42.2 6.8 %shard_map.105 = (bf16[256,1024]{1,0:T(8,128)(2,1)S(1)}, bf16[2,64,1024]{2,1,0:T(8,128)(2,1)S(1)}) custom-call(bf16[256,1024]{1,0:T(8,128)(2,1)S(1)} %collective-permute-done.1.partner_q.q_ref, f32[2,8,256,128]{3,2,1,0:T(8,128)S(1)} %get-tuple-element.25.acc_ref, f32[2,256,128]{2,1,0:T(8,128)S(1)} %get-tuple-element.26.stat_ref, ...), custom_call_target="tpu_custom_call" | custom-call | flops 2147483648 | bytes 4194304 | tf_op jit(solution)/shard_map/pallas_call | solution.py:334
  49.0 0.6 collective-permute-start.13
  49.5 4.8 %collective-permute-start.18 = (bf16[256,1024]{1,0:T(8,128)(2,1)S(1)}, bf16[256,1024]{1,0:T(8,128)(2,1)S(1)}, u32[]{:S(2)}, u32[]{:S(2)}) collective-permute-start(bf16[256,1024]{1,0:T(8,128)(2,1)S(1)} %get-tuple-element.36), channel_id=1, source_target_pairs={{0,64},{16,80},{32,96},{48,112},{64,0},{80,16},{96,32},{112,48},{1... | collective-permute-start | bytes 1572872 | tf_op jit(solution)/shard_map/ppermute | solution.py:356
  54.3 0.1 pad_maximum_fusion.2
  54.4 1.6 %collective-permute-start.14 = (bf16[2,64,1024]{2,1,0:T(8,128)(2,1)S(1)}, bf16[2,64,1024]{2,1,0:T(8,128)(2,1)S(1)}, u32[]{:S(2)}, u32[]{:S(2)}) collective-permute-start(bf16[2,64,1024]{2,1,0:T(8,128)(2,1)S(1)} %get-tuple-element.28._), channel_id=1, source_target_pairs={{0,12},{2,14},{4,0},{6,2},{8,4},{10,6},{12,8},{14,10},{1,13},{3,15... | collective-permute-start | bytes 786440 | tf_op jit(solution)/shard_map/ppermute | solution.py:364
  56.0 1.4 %collective-permute-start.15 = (bf16[2,64,1024]{2,1,0:T(8,128)(2,1)S(1)}, bf16[2,64,1024]{2,1,0:T(8,128)(2,1)S(1)}, u32[]{:S(2)}, u32[]{:S(2)}) collective-permute-start(bf16[2,64,1024]{2,1,0:T(8,128)(2,1)S(1)} %get-tuple-element.28._), channel_id=1, source_target_pairs={{0,8},{2,10},{4,12},{6,14},{8,0},{10,2},{12,4},{14,6},{1,9},{3,11}... | collective-permute-start | bytes 786440 | tf_op jit(solution)/shard_map/ppermute | solution.py:364
  57.4 1.1 %shard_map.106 = (bf16[64,1152]{1,0:T(8,128)(2,1)S(1)}, bf16[64,1152]{1,0:T(8,128)(2,1)S(1)}, f32[8,128]{1,0:T(8,128)S(1)}) custom-call(s32[2,16]{1,0:T(2,128)S(1)} %copy-done.4, bf16[2,64,1024]{2,1,0:T(8,128)(2,1)S(1)} %get-tuple-element.28._, bf16[64,1024]{1,0:T(8,128)(2,1)S(1)} %collective-permute-done.11.rows0_ref, ...), custom_call_target="tpu_custom_call" | custom-call | flops 2147483648 | bytes 3145728 | tf_op jit(solution)/shard_map/pallas_call | solution.py:334
  58.6 6.2 %collective-permute-start.16 = (bf16[64,1152]{1,0:T(8,128)(2,1)S(1)}, bf16[64,1152]{1,0:T(8,128)(2,1)S(1)}, u32[]{:S(2)}, u32[]{:S(2)}) collective-permute-start(bf16[64,1152]{1,0:T(8,128)(2,1)S(1)} %get-tuple-element.34), channel_id=1, source_target_pairs={{0,1},{1,0},{16,17},{17,16},{32,33},{33,32},{48,49},{49,48},{64,65... | collective-permute-start | bytes 442376 | tf_op jit(solution)/shard_map/ppermute | solution.py:369
  64.8 4.5 %collective-permute-start.17 = (bf16[64,1152]{1,0:T(8,128)(2,1)S(1)}, bf16[64,1152]{1,0:T(8,128)(2,1)S(1)}, u32[]{:S(2)}, u32[]{:S(2)}) collective-permute-start(bf16[64,1152]{1,0:T(8,128)(2,1)S(1)} %get-tuple-element.35), channel_id=1, source_target_pairs={{0,65},{1,64},{16,81},{17,80},{32,97},{33,96},{48,113},{49,112},{6... | collective-permute-start | bytes 442376 | tf_op jit(solution)/shard_map/ppermute | solution.py:369
  69.3 7.4 %shard_map.107 = (bf16[2,256,1024]{2,1,0:T(8,128)(2,1)}, f32[8,128]{1,0:T(8,128)S(1)}) custom-call(bf16[2,256,1024]{2,1,0:T(8,128)(2,1)S(1)} %bitcast.22, f32[2,8,256,128]{3,2,1,0:T(8,128)S(1)} %get-tuple-element.25.acc_ref, f32[2,256,128]{2,1,0:T(8,128)S(1)} %get-tuple-element.26.stat_ref, bf16[2,256,256]{2,1,0:T(8,128)(2,1)S(1)} %pad_maximum_fusion.1.refs_0_.refs_4_, ...), custom_call_target="tpu_custom_call" | custom-call | flops 2147483648 | bytes 4194304 | tf_op jit(solution)/shard_map/pallas_call | solution.py:334
  76.8 4.1 %shard_map.108 = (f32[64,1024]{1,0:T(8,128)S(1)}, f32[64,1024]{1,0:T(8,128)S(1)}) custom-call(s32[16]{0:T(128)S(1)} %bitcast.24, f32[8,128]{1,0:T(8,128)S(1)} %get-tuple-element.31._, f32[64,128]{1,0:T(8,128)S(1)} %get-tuple-element.46.cos_ref, f32[64,128]{1,0:T(8,128)S(1)} %get-tuple-element.47.sin_ref, f32[1,8192]{1,0:T(1,128)S(1)} %bitcast.23, ...), custom_call_target="tpu_custom_call" | custom-call | flops 268435456 | bytes 8388608 | tf_op jit(solution)/shard_map/pallas_call | solution.py:334
  80.9 2.0 %shard_map.109 = (bf16[16,4,1024]{2,1,0:T(4,128)(2,1)}, bf16[2,256,1024]{2,1,0:T(8,128)(2,1)}) custom-call(s32[2,16]{1,0:T(2,128)S(1)} %copy-done.4, f32[64,1024]{1,0:T(8,128)S(1)} %get-tuple-element.32.local_ref, f32[64,1024]{1,0:T(8,128)S(1)} %get-tuple-element.33.level_ref, ...), custom_call_target="tpu_custom_call", output_to_operand_aliasing={{1}: (6, {})} | custom-call | flops 524288 | bytes 1048576 | tf_op jit(solution)/shard_map/pallas_call | solution.py:334
  (38 shorter events, 0.2 us)
Async XLA Ops:
  0.6 28.9 %copy-start.2 = (bf16[1,2,256,1024]{3,2,1,0:T(8,128)(2,1)S(1)}, bf16[1,2,256,1024]{3,2,1,0:T(8,128)(2,1)}, u32[]{:S(2)}) copy-start(bf16[1,2,256,1024]{3,2,1,0:T(8,128)(2,1)} %param.9) | copy-start | bytes 3145732
  0.6 11.7 %copy-start.5 = (s32[1,1,16]{2,1,0:T(1,128)S(1)}, s32[1,1,16]{2,1,0:T(1,128)}, u32[]{:S(2)}) copy-start(s32[1,1,16]{2,1,0:T(1,128)} %param.17) | copy-start | bytes 196
  0.7 28.9 %copy-start.6 = (bf16[1,1,16,4,1024]{4,3,2,1,0:T(4,128)(2,1)S(1)}, bf16[1,1,16,4,1024]{4,3,2,1,0:T(4,128)(2,1)}, u32[]{:S(2)}) copy-start(bf16[1,1,16,4,1024]{4,3,2,1,0:T(4,128)(2,1)} %param.13) | copy-start | bytes 393220
  0.7 28.9 %copy-start.7 = (bf16[1,1,16,4,1024]{4,3,2,1,0:T(4,128)(2,1)S(1)}, bf16[1,1,16,4,1024]{4,3,2,1,0:T(4,128)(2,1)}, u32[]{:S(2)}) copy-start(bf16[1,1,16,4,1024]{4,3,2,1,0:T(4,128)(2,1)} %param.11) | copy-start | bytes 393220
  1.8 7.5 %collective-permute-start = (bf16[256,256]{1,0:T(8,128)(2,1)S(1)}, bf16[256,256]{1,0:T(8,128)(2,1)S(1)}, u32[]{:S(2)}, u32[]{:S(2)}) collective-permute-start(bf16[256,256]{1,0:T(8,128)(2,1)S(1)} %get-tuple-element.42), channel_id=1, source_target_pairs={{0,64},{16,80},{32,96},{48,112},{64,0},{80,16},{96,32},{112,48},{1... | collective-permute-start | bytes 393224 | tf_op jit(solution)/shard_map/ppermute | solution.py:356
  3.8 11.8 %collective-permute-start.6 = (bf16[256,256]{1,0:T(8,128)(2,1)S(1)}, bf16[256,256]{1,0:T(8,128)(2,1)}, u32[]{:S(2)}, u32[]{:S(2)}) collective-permute-start(bf16[256,256]{1,0:T(8,128)(2,1)S(1)} %get-tuple-element.42), channel_id=1, source_target_pairs={{0,192},{16,208},{32,224},{48,240},{64,128},{80,144},{96,160},{112... | collective-permute-start | bytes 393224 | tf_op jit(solution)/shard_map/ppermute | solution.py:356
  3.8 14.9 %collective-permute-start.5 = (bf16[256,256]{1,0:T(8,128)(2,1)S(1)}, bf16[256,256]{1,0:T(8,128)(2,1)}, u32[]{:S(2)}, u32[]{:S(2)}) collective-permute-start(bf16[256,256]{1,0:T(8,128)(2,1)S(1)} %get-tuple-element.40), channel_id=1, source_target_pairs={{0,128},{16,144},{32,160},{48,176},{64,192},{80,208},{96,224},{112... | collective-permute-start | bytes 393224 | tf_op jit(solution)/shard_map/ppermute | solution.py:356
  9.3 20.3 %collective-permute-start.1 = (bf16[256,1024]{1,0:T(8,128)(2,1)S(1)}, bf16[256,1024]{1,0:T(8,128)(2,1)S(1)}, u32[]{:S(2)}, u32[]{:S(2)}) collective-permute-start(bf16[256,1024]{1,0:T(8,128)(2,1)S(1)} %dynamic-slice_bitcast_fusion), channel_id=1, source_target_pairs={{0,64},{16,80},{32,96},{48,112},{64,0},{80,16},{96,32},{112,48},{1... | collective-permute-start | bytes 1572872 | tf_op jit(solution)/shard_map/ppermute | solution.py:356
  12.3 10.7 %collective-permute-start.2 = (bf16[2,256,256]{2,1,0:T(8,128)(2,1)S(1)}, bf16[2,256,256]{2,1,0:T(8,128)(2,1)S(1)}, u32[]{:S(2)}, u32[]{:S(2)}) collective-permute-start(bf16[2,256,256]{2,1,0:T(8,128)(2,1)S(1)} %pad_maximum_fusion.refs_0_), channel_id=1, source_target_pairs={{0,16},{16,32},{32,48},{48,0},{64,80},{80,96},{96,112},{112,64},{1... | collective-permute-start | bytes 786440 | tf_op jit(solution)/shard_map/ppermute | solution.py:352
  13.9 10.5 %collective-permute-start.3 = (bf16[2,256,256]{2,1,0:T(8,128)(2,1)S(1)}, bf16[2,256,256]{2,1,0:T(8,128)(2,1)S(1)}, u32[]{:S(2)}, u32[]{:S(2)}) collective-permute-start(bf16[2,256,256]{2,1,0:T(8,128)(2,1)S(1)} %pad_maximum_fusion.refs_0_), channel_id=1, source_target_pairs={{0,48},{16,0},{32,16},{48,32},{64,112},{80,64},{96,80},{112,96},{1... | collective-permute-start | bytes 786440 | tf_op jit(solution)/shard_map/ppermute | solution.py:352
  15.6 14.0 %collective-permute-start.4 = (bf16[2,256,256]{2,1,0:T(8,128)(2,1)S(1)}, bf16[2,256,256]{2,1,0:T(8,128)(2,1)S(1)}, u32[]{:S(2)}, u32[]{:S(2)}) collective-permute-start(bf16[2,256,256]{2,1,0:T(8,128)(2,1)S(1)} %pad_maximum_fusion.refs_0_), channel_id=1, source_target_pairs={{0,32},{16,48},{32,0},{48,16},{64,96},{80,112},{96,64},{112,80},{1... | collective-permute-start | bytes 786440 | tf_op jit(solution)/shard_map/ppermute | solution.py:352
  19.7 22.4 %collective-permute-start.7 = (bf16[2,256,256]{2,1,0:T(8,128)(2,1)S(1)}, bf16[2,256,256]{2,1,0:T(8,128)(2,1)S(1)}, u32[]{:S(2)}, u32[]{:S(2)}) collective-permute-start(bf16[2,256,256]{2,1,0:T(8,128)(2,1)S(1)} %pad_maximum_fusion.1.refs_0_.refs_4_), channel_id=1, source_target_pairs={{0,16},{16,32},{32,48},{48,0},{64,80},{80,96},{96,112},{112,64},{1... | collective-permute-start | bytes 786440 | tf_op jit(solution)/shard_map/ppermute | solution.py:352
  23.0 19.2 %collective-permute-start.8 = (bf16[2,256,256]{2,1,0:T(8,128)(2,1)S(1)}, bf16[2,256,256]{2,1,0:T(8,128)(2,1)S(1)}, u32[]{:S(2)}, u32[]{:S(2)}) collective-permute-start(bf16[2,256,256]{2,1,0:T(8,128)(2,1)S(1)} %pad_maximum_fusion.1.refs_0_.refs_4_), channel_id=1, source_target_pairs={{0,48},{16,0},{32,16},{48,32},{64,112},{80,64},{96,80},{112,96},{1... | collective-permute-start | bytes 786440 | tf_op jit(solution)/shard_map/ppermute | solution.py:352
  24.4 17.7 %collective-permute-start.9 = (bf16[2,256,256]{2,1,0:T(8,128)(2,1)S(1)}, bf16[2,256,256]{2,1,0:T(8,128)(2,1)S(1)}, u32[]{:S(2)}, u32[]{:S(2)}) collective-permute-start(bf16[2,256,256]{2,1,0:T(8,128)(2,1)S(1)} %pad_maximum_fusion.1.refs_0_.refs_4_), channel_id=1, source_target_pairs={{0,32},{16,48},{32,0},{48,16},{64,96},{80,112},{96,64},{112,80},{1... | collective-permute-start | bytes 786440 | tf_op jit(solution)/shard_map/ppermute | solution.py:352
  39.9 2.3 %collective-permute-start.10 = (bf16[64,1024]{1,0:T(8,128)(2,1)S(1)}, bf16[64,1024]{1,0:T(8,128)(2,1)S(1)}, u32[]{:S(2)}, u32[]{:S(2)}) collective-permute-start(bf16[64,1024]{1,0:T(8,128)(2,1)S(1)} %get-tuple-element.27.refs_4_.own_ref), channel_id=1, source_target_pairs={{0,2},{2,0},{4,6},{6,4},{8,10},{10,8},{12,14},{14,12},{1,3},{3,1},... | collective-permute-start | bytes 393224 | tf_op jit(solution)/shard_map/ppermute | solution.py:424
  40.4 15.7 %collective-permute-start.11 = (bf16[64,1024]{1,0:T(8,128)(2,1)S(1)}, bf16[64,1024]{1,0:T(8,128)(2,1)S(1)}, u32[]{:S(2)}, u32[]{:S(2)}) collective-permute-start(bf16[64,1024]{1,0:T(8,128)(2,1)S(1)} %get-tuple-element.29.q_ref), channel_id=1, source_target_pairs={{0,1},{1,0},{16,17},{17,16},{32,33},{33,32},{48,49},{49,48},{64,65... | collective-permute-start | bytes 393224 | tf_op jit(solution)/shard_map/ppermute | solution.py:369
  42.1 15.3 %collective-permute-start.12 = (bf16[64,1024]{1,0:T(8,128)(2,1)S(1)}, bf16[64,1024]{1,0:T(8,128)(2,1)S(1)}, u32[]{:S(2)}, u32[]{:S(2)}) collective-permute-start(bf16[64,1024]{1,0:T(8,128)(2,1)S(1)} %get-tuple-element.29.q_ref), channel_id=1, source_target_pairs={{0,65},{1,64},{16,81},{17,80},{32,97},{33,96},{48,113},{49,112},{6... | collective-permute-start | bytes 393224 | tf_op jit(solution)/shard_map/ppermute | solution.py:369
  42.2 15.3 %copy-start.4 = (s32[2,16]{1,0:T(2,128)S(1)}, s32[2,16]{1,0:T(2,128)}, u32[]{:S(2)}) copy-start(s32[2,16]{1,0:T(2,128)} %prompt_ref.3) | copy-start | bytes 388
  49.0 15.8 %collective-permute-start.13 = (bf16[2,64,1024]{2,1,0:T(8,128)(2,1)S(1)}, bf16[2,64,1024]{2,1,0:T(8,128)(2,1)S(1)}, u32[]{:S(2)}, u32[]{:S(2)}) collective-permute-start(bf16[2,64,1024]{2,1,0:T(8,128)(2,1)S(1)} %get-tuple-element.28._), channel_id=1, source_target_pairs={{0,4},{2,6},{4,8},{6,10},{8,12},{10,14},{12,0},{14,2},{1,5},{3,7},... | collective-permute-start | bytes 786440 | tf_op jit(solution)/shard_map/ppermute | solution.py:364
  49.5 31.4 %collective-permute-start.18 = (bf16[256,1024]{1,0:T(8,128)(2,1)S(1)}, bf16[256,1024]{1,0:T(8,128)(2,1)S(1)}, u32[]{:S(2)}, u32[]{:S(2)}) collective-permute-start(bf16[256,1024]{1,0:T(8,128)(2,1)S(1)} %get-tuple-element.36), channel_id=1, source_target_pairs={{0,64},{16,80},{32,96},{48,112},{64,0},{80,16},{96,32},{112,48},{1... | collective-permute-start | bytes 1572872 | tf_op jit(solution)/shard_map/ppermute | solution.py:356
  54.4 22.3 %collective-permute-start.14 = (bf16[2,64,1024]{2,1,0:T(8,128)(2,1)S(1)}, bf16[2,64,1024]{2,1,0:T(8,128)(2,1)S(1)}, u32[]{:S(2)}, u32[]{:S(2)}) collective-permute-start(bf16[2,64,1024]{2,1,0:T(8,128)(2,1)S(1)} %get-tuple-element.28._), channel_id=1, source_target_pairs={{0,12},{2,14},{4,0},{6,2},{8,4},{10,6},{12,8},{14,10},{1,13},{3,15... | collective-permute-start | bytes 786440 | tf_op jit(solution)/shard_map/ppermute | solution.py:364
  56.0 20.7 %collective-permute-start.15 = (bf16[2,64,1024]{2,1,0:T(8,128)(2,1)S(1)}, bf16[2,64,1024]{2,1,0:T(8,128)(2,1)S(1)}, u32[]{:S(2)}, u32[]{:S(2)}) collective-permute-start(bf16[2,64,1024]{2,1,0:T(8,128)(2,1)S(1)} %get-tuple-element.28._), channel_id=1, source_target_pairs={{0,8},{2,10},{4,12},{6,14},{8,0},{10,2},{12,4},{14,6},{1,9},{3,11}... | collective-permute-start | bytes 786440 | tf_op jit(solution)/shard_map/ppermute | solution.py:364
  58.6 22.3 %collective-permute-start.16 = (bf16[64,1152]{1,0:T(8,128)(2,1)S(1)}, bf16[64,1152]{1,0:T(8,128)(2,1)S(1)}, u32[]{:S(2)}, u32[]{:S(2)}) collective-permute-start(bf16[64,1152]{1,0:T(8,128)(2,1)S(1)} %get-tuple-element.34), channel_id=1, source_target_pairs={{0,1},{1,0},{16,17},{17,16},{32,33},{33,32},{48,49},{49,48},{64,65... | collective-permute-start | bytes 442376 | tf_op jit(solution)/shard_map/ppermute | solution.py:369
  64.8 16.1 %collective-permute-start.17 = (bf16[64,1152]{1,0:T(8,128)(2,1)S(1)}, bf16[64,1152]{1,0:T(8,128)(2,1)S(1)}, u32[]{:S(2)}, u32[]{:S(2)}) collective-permute-start(bf16[64,1152]{1,0:T(8,128)(2,1)S(1)} %get-tuple-element.35), channel_id=1, source_target_pairs={{0,65},{1,64},{16,81},{17,80},{32,97},{33,96},{48,113},{49,112},{6... | collective-permute-start | bytes 442376 | tf_op jit(solution)/shard_map/ppermute | solution.py:369
  69.3 7.5 %copy-start = (bf16[8192,256]{1,0:T(8,128)(2,1)S(1)}, bf16[8192,256]{1,0:T(8,128)(2,1)}, u32[]{:S(2)}) copy-start(bf16[8192,256]{1,0:T(8,128)(2,1)} %refs_3_.1) | copy-start | bytes 12582916
  69.3 7.5 %copy-start.1 = (bf16[1,1,16,256,256]{4,3,2,1,0:T(8,128)(2,1)S(1)}, bf16[1,1,16,256,256]{4,3,2,1,0:T(8,128)(2,1)}, u32[]{:S(2)}) copy-start(bf16[1,1,16,256,256]{4,3,2,1,0:T(8,128)(2,1)} %param.12) | copy-start | bytes 6291460
  69.3 7.5 %copy-start.3 = (f32[8192]{0:T(1024)S(1)}, f32[8192]{0:T(1024)}, u32[]{:S(2)}) copy-start(f32[8192]{0:T(1024)} %param.14) | copy-start | bytes 98308
